TPU v7x, 32 devices: a whole 2x2x4 slice. The times are simulated.
32 devices in a mesh: ctx: 16 (over z, y, x), chan: 2 (over core).
Axes of the slice: x: 2, y: 2, z: 4, core: 2. Of those that a mesh axis runs over, the one named last changes fastest.
Arguments:
- tokens: bfloat16 [131072, 512], P('ctx', 'chan'), parts along dimension 1, may hold values from -6 to 6
- conv_taps: float32 [3, 512], P(None, 'chan'), parts along dimension 1, may hold values from -3 to 3
- gate_weight: bfloat16 [512, 256], P('chan'), parts along dimension 0, may hold values from -0.375 to 0.375
- row_factor: bfloat16 [256, 512, 512], P('ctx'), may hold values from -1 to 2
- col_factor: bfloat16 [512, 256, 256], P('ctx'), may hold values from -1 to 2
- cotangent: bfloat16 [512, 256, 512], P('ctx', None, 'chan'), parts along dimension 2, may hold values from -0.0390625 to 0.0390625
Outputs:
- mixed: bfloat16 [512, 256, 512], P('ctx', None, 'chan'), parts along dimension 2
- conv_grad: float32 [3, 512], P(None, 'chan'), parts along dimension 1
- gate_grad: float32 [512, 256], P('chan'), parts along dimension 0
There are 2 independent parts, one for each index of `chan`. A program takes and returns all parts, laid end to end along the dimension named above; an argument that names none is the same for every part. Nothing has to cross between parts.
All inputs are finite; a program needn't handle non-finite values.
Results may differ from a plain program's by a relative error of at most 0.0057.
Values may be sent and summed in bfloat16 or wider, within the bound.
No kernel may reach another device: no remote copies, remote signals or barrier semaphores. Data moves between devices by JAX's collectives and lax.ppermute only.
A program may use at most 128 MiB of HBM per device.

v0:
```python
import jax
import jax.numpy as jnp
from jax import lax
from jax.sharding import PartitionSpec as P


def padded_2(block, sides, width):
    for axis, dim in sides:
        count = lax.axis_size(axis)
        forward = [(i, i + 1) for i in range(count - 1)]
        backward = [(target, source) for source, target in forward]
        low = lax.ppermute(
            lax.slice_in_dim(block, block.shape[dim] - width, None, axis=dim), axis, forward
        )
        high = lax.ppermute(lax.slice_in_dim(block, 0, width, axis=dim), axis, backward)
        block = jnp.concatenate([low, block, high], axis=dim)
    return block


def local(tokens, conv_taps, gate_weight, row_factor, col_factor, cotangent):
    count = tokens.shape[0]
    width = tokens.shape[1]
    run_rows = row_factor.shape[0]
    run_len = row_factor.shape[1]
    padded = padded_2(tokens, (("ctx", 0),), 1)
    conv = (
        conv_taps[0] * padded[0:count]
        + conv_taps[1] * padded[1 : count + 1]
        + conv_taps[2] * padded[2 : count + 2]
    )
    gate = jnp.dot(tokens, gate_weight, preferred_element_type=jnp.float32)
    sig = jax.nn.sigmoid(gate)
    gated = (conv * sig).astype(jnp.bfloat16).reshape(run_rows, run_len, width)
    first = jnp.einsum(
        "rdc,rck->rdk", row_factor, gated, preferred_element_type=jnp.float32
    ).astype(jnp.bfloat16)
    back_first = jnp.einsum(
        "dqr,dqk->rdk", col_factor, cotangent, preferred_element_type=jnp.float32
    ).astype(jnp.bfloat16)
    mixed = jnp.einsum(
        "dqr,rdk->dqk",
        col_factor,
        lax.all_to_all(first, "ctx", split_axis=1, concat_axis=0, tiled=True),
        preferred_element_type=jnp.float32,
    ).astype(jnp.bfloat16)
    back_gated = jnp.einsum(
        "rdc,rdk->rck",
        row_factor,
        lax.all_to_all(back_first, "ctx", split_axis=0, concat_axis=1, tiled=True),
        preferred_element_type=jnp.float32,
    )
    back_gated = back_gated.reshape(count, width)
    back_conv = back_gated * sig
    back_gate = (back_gated * conv * sig * (1.0 - sig)).astype(jnp.bfloat16)
    conv_part = jnp.stack(
        [jnp.sum(back_conv * padded[j : j + count].astype(jnp.float32), axis=0) for j in range(3)]
    )
    gate_part = lax.dot_general(
        tokens, back_gate, (((0,), (0,)), ((), ())), preferred_element_type=jnp.float32
    )
    conv_grad, gate_grad = lax.psum((conv_part, gate_part), "ctx")
    return (mixed, conv_grad, gate_grad)


def solution(mesh):
    placed = (
        P("ctx", "chan"),
        P(None, "chan"),
        P("chan", None),
        P("ctx", None, None),
        P("ctx", None, None),
        P("ctx", None, "chan"),
    )
    return jax.shard_map(
        local,
        mesh=mesh,
        in_specs=placed,
        out_specs=(P("ctx", None, "chan"), P(None, "chan"), P("chan", None)),
        check_vma=False,
    )
```

profile of v0, /device:TPU:0, one launch (start us, length us, event | category | flops | bytes accessed | tf_op | source)
XLA Modules:
  0.0 368.6 jit_solution(11533662008699973095)
XLA Ops:
  7.2 0.0 copy-start
  7.2 6.8 %convert_bitcast_fusion = bf16[256,32,256]{0,2,1:T(8,128)(2,1)} fusion(bf16[32,256,256]{2,1,0:T(8,128)(2,1)} %param.11, bf16[32,256,256]{2,1,0:T(8,128)(2,1)} %param.10), kind=kOutput, calls=%fused_computation.25 | convolution fusion | flops 1075838976 | bytes 12582912 | tf_op jit(solution)/shard_map/dqr,dqk->rdk/dot_general | solution.py:37
  14.0 7.9 %copy.33 = bf16[256,32,256]{2,1,0:T(8,128)(2,1)} copy(bf16[256,32,256]{0,2,1:T(8,128)(2,1)} %convert_bitcast_fusion) | data formatting | bytes 8388608 | tf_op jit(solution)/shard_map/convert_element_type | solution.py:39
  21.9 8.5 %all-to-all-start.1 = ((bf16[256,32,256]{2,1,0:T(8,128)(2,1)}), bf16[256,32,256]{2,1,0:T(8,128)(2,1)}, u32[]{:S(2)}, u32[]{:S(2)}) async-start(bf16[256,32,256]{2,1,0:T(8,128)(2,1)} %copy.33), calls=%async_computation.1 | async-start | bytes 8388608 | tf_op jit(solution)/shard_map/all_to_all | solution.py:49
  30.4 0.7 fusion.15
  31.2 3.8 %collective-permute-start = (bf16[1,256]{1,0:T(2,128)(2,1)S(1)}, bf16[1,256]{1,0:T(2,128)(2,1)S(1)}, u32[]{:S(2)}, u32[]{:S(2)}) collective-permute-start(bf16[1,256]{1,0:T(2,128)(2,1)S(1)} %get-tuple-element.17), channel_id=1, source_target_pairs={{0,2},{2,4},{4,6},{6,8},{8,10},{10,12},{12,14},{14,16},{16,18},{18... | collective-permute-start | bytes 1544 | tf_op jit(solution)/shard_map/ppermute | solution.py:12
  34.9 1.5 collective-permute-start.1
  36.4 0.0 copy-done.3
  36.4 73.7 %all-to-all-done.1 = bf16[256,32,256]{2,1,0:T(8,128)(2,1)} async-done(((bf16[256,32,256]{2,1,0:T(8,128)(2,1)}), bf16[256,32,256]{2,1,0:T(8,128)(2,1)}, u32[]{:S(2)}, u32[]{:S(2)}) %all-to-all-start.1) | async-done | bytes 4194336 | tf_op jit(solution)/shard_map/all_to_all | solution.py:49
  110.2 2.6 copy.34
  112.8 9.0 %convolution_bitcast_fusion = f32[16,512,256]{1,2,0:T(8,128)} fusion(bf16[16,512,256]{2,1,0:T(8,128)(2,1)S(1)} %bitcast.51, bf16[16,512,512]{2,1,0:T(8,128)(2,1)} %param.9), kind=kOutput, calls=%fused_computation.28 | convolution fusion | flops 2147483648 | bytes 20971520 | tf_op jit(solution)/shard_map/rdc,rdk->rck/dot_general | solution.py:46
  121.8 9.3 %copy.36 = f32[16,512,256]{2,1,0:T(8,128)} copy(f32[16,512,256]{1,2,0:T(8,128)} %convolution_bitcast_fusion) | data formatting | bytes 16777216 | tf_op jit(solution)/shard_map/rdc,rdk->rck/dot_general | solution.py:46
  131.0 0.0 collective-permute-done
  131.0 0.0 collective-permute-done.1
  131.0 0.0 copy-done
  131.1 17.3 %fusion.5 = (f32[256]{0:T(256)S(1)}, f32[256]{0:T(256)S(1)}, f32[256]{0:T(256)S(1)}, bf16[8192,256]{1,0:T(8,128)(2,1)}, bf16[8192,256]{1,0:T(8,128)(2,1)}) fusion(bf16[8192,256]{1,0:T(8,128)(2,1)} %param.6, bf16[1,256]{1,0:T(2,128)(2,1)S(1)} %collective-permute-done, f32[16,512,256]{2,1,0:T(8,128)} %copy.36, bf16[1,256]{1,0:T(2,128)(2,1)S(1)} %collective-permute-done.1, ...), kind=kOutput, calls=%fused_computation.12 | convolution fusion | flops 1138752768 | bytes 21109760 | tf_op jit(solution)/shard_map/dot_general | solution.py:31
  148.3 9.1 %convert_bitcast_fusion.2 = bf16[16,512,256]{1,2,0:T(8,128)(2,1)} fusion(bf16[16,512,256]{2,1,0:T(8,128)(2,1)} %bitcast.53, bf16[16,512,512]{2,1,0:T(8,128)(2,1)} %param.9), kind=kOutput, calls=%fused_computation.27 | convolution fusion | flops 2149580800 | bytes 16777216 | tf_op jit(solution)/shard_map/rdc,rck->rdk/dot_general | solution.py:34
  157.4 7.9 %copy.28 = bf16[16,512,256]{2,0,1:T(8,128)(2,1)} copy(bf16[16,512,256]{1,2,0:T(8,128)(2,1)} %convert_bitcast_fusion.2) | data formatting | bytes 8388608 | tf_op jit(solution)/shard_map/convert_element_type | solution.py:36
  165.2 20.1 %all-to-all-start = ((bf16[16,512,256]{2,0,1:T(8,128)(2,1)}), bf16[16,512,256]{2,0,1:T(8,128)(2,1)}, u32[]{:S(2)}, u32[]{:S(2)}) async-start(bf16[16,512,256]{2,0,1:T(8,128)(2,1)} %copy.28), calls=%async_computation | async-start | bytes 8388608 | tf_op jit(solution)/shard_map/all_to_all | solution.py:43
  185.3 0.3 all-reduce.2.cloned.1.call-start
  185.6 5.5 %convolution_bitcast_fusion.1 = f32[256,256]{0,1:T(8,128)} fusion(bf16[8192,256]{1,0:T(8,128)(2,1)} %get-tuple-element.15, bf16[8192,256]{1,0:T(8,128)(2,1)} %param.6), kind=kOutput, calls=%fused_computation.29 | convolution fusion | flops 1073741824 | bytes 8650752 | tf_op jit(solution)/shard_map/dot_general | solution.py:58
  191.0 0.0 all-reduce.2.cloned.1.call-update
  191.1 100.1 %psum.14 = f32[3,256]{1,0:T(4,128)} all-reduce(f32[3,256]{1,0:T(4,128)S(1)} %pad_maximum_fusion.2), channel_id=1, replica_groups=mesh['ctx'=16,'chan'=2] {'ctx'}, use_global_device_ids=true, to_apply=%region_3.0 | all-reduce | flops 768 | bytes 6144 | tf_op jit(solution)/shard_map/psum | solution.py:61
  291.1 51.3 %all-reduce.2.cloned.1.call-done = f32[256,256]{0,1:T(8,128)} async-done(((f32[256,256]{0,1:T(8,128)}), f32[256,256]{0,1:T(8,128)}) %all-reduce.2.cloned.1.call-update) | async-done | bytes 262160 | tf_op jit(solution)/shard_map/psum | solution.py:61
  342.5 1.8 copy.38
  344.2 0.0 all-to-all-done
  344.2 4.1 %copy.30 = bf16[16,16,32,256]{3,2,1,0:T(8,128)(2,1)S(1)} copy(bf16[16,16,32,256]{3,1,2,0:T(8,128)(2,1)} %bitcast.7) | data formatting | bytes 8388608 | tf_op jit(solution)/shard_map/all_to_all | solution.py:43
  348.4 0.0 copy-done.2
  348.4 0.0 copy-start.1
  348.4 7.0 %convert_bitcast_fusion.1 = bf16[32,256,256]{1,2,0:T(8,128)(2,1)} fusion(bf16[32,256,256]{2,1,0:T(8,128)(2,1)S(1)} %copy-done.2, bf16[256,32,256]{2,1,0:T(8,128)(2,1)S(1)} %bitcast.52), kind=kOutput, calls=%fused_computation.26 | convolution fusion | flops 1075838976 | bytes 12582912 | tf_op jit(solution)/shard_map/dqr,rdk->dqk/dot_general | solution.py:40
  355.4 6.4 %copy.37 = bf16[32,256,256]{2,1,0:T(8,128)(2,1)} copy(bf16[32,256,256]{1,2,0:T(8,128)(2,1)} %convert_bitcast_fusion.1) | data formatting | bytes 8388608
  361.8 0.0 copy-done.1
  (4 shorter events, 0.0 us)
Async XLA Ops:
  7.2 123.9 %copy-start = (bf16[256,256]{1,0:T(8,128)(2,1)S(1)}, bf16[256,256]{1,0:T(8,128)(2,1)}, u32[]{:S(2)}) copy-start(bf16[256,256]{1,0:T(8,128)(2,1)} %param.8) | copy-start | bytes 393220
  21.9 14.5 %copy-start.3 = (f32[3,256]{1,0:T(4,128)S(1)}, f32[3,256]{1,0:T(4,128)}, u32[]{:S(2)}) copy-start(f32[3,256]{1,0:T(4,128)} %param.7) | copy-start | bytes 9220
  21.9 88.2 %all-to-all-start.1 = ((bf16[256,32,256]{2,1,0:T(8,128)(2,1)}), bf16[256,32,256]{2,1,0:T(8,128)(2,1)}, u32[]{:S(2)}, u32[]{:S(2)}) async-start(bf16[256,32,256]{2,1,0:T(8,128)(2,1)} %copy.33), calls=%async_computation.1 | async-start | bytes 8388608 | tf_op jit(solution)/shard_map/all_to_all | solution.py:49
  31.2 99.9 %collective-permute-start = (bf16[1,256]{1,0:T(2,128)(2,1)S(1)}, bf16[1,256]{1,0:T(2,128)(2,1)S(1)}, u32[]{:S(2)}, u32[]{:S(2)}) collective-permute-start(bf16[1,256]{1,0:T(2,128)(2,1)S(1)} %get-tuple-element.17), channel_id=1, source_target_pairs={{0,2},{2,4},{4,6},{6,8},{8,10},{10,12},{12,14},{14,16},{16,18},{18... | collective-permute-start | bytes 1544 | tf_op jit(solution)/shard_map/ppermute | solution.py:12
  34.9 96.1 %collective-permute-start.1 = (bf16[1,256]{1,0:T(2,128)(2,1)S(1)}, bf16[1,256]{1,0:T(2,128)(2,1)S(1)}, u32[]{:S(2)}, u32[]{:S(2)}) collective-permute-start(bf16[1,256]{1,0:T(2,128)(2,1)S(1)} %get-tuple-element.18), channel_id=1, source_target_pairs={{2,0},{4,2},{6,4},{8,6},{10,8},{12,10},{14,12},{16,14},{18,16},{20... | collective-permute-start | bytes 1544 | tf_op jit(solution)/shard_map/ppermute | solution.py:15
  165.2 179.0 %all-to-all-start = ((bf16[16,512,256]{2,0,1:T(8,128)(2,1)}), bf16[16,512,256]{2,0,1:T(8,128)(2,1)}, u32[]{:S(2)}, u32[]{:S(2)}) async-start(bf16[16,512,256]{2,0,1:T(8,128)(2,1)} %copy.28), calls=%async_computation | async-start | bytes 8388608 | tf_op jit(solution)/shard_map/all_to_all | solution.py:43
  185.3 157.2 %all-reduce.2.cloned.1.call-start = ((), (), s32[]{:S(2)}) async-start(), calls=%async_computation.2 | async-start | bytes 524288 | tf_op jit(solution)/shard_map/psum | solution.py:61
  344.2 4.1 %copy-start.2 = (bf16[32,256,256]{2,1,0:T(8,128)(2,1)S(1)}, bf16[32,256,256]{2,1,0:T(8,128)(2,1)}, u32[]{:S(2)}) copy-start(bf16[32,256,256]{2,1,0:T(8,128)(2,1)} %param.10) | copy-start | bytes 12582916
  348.4 13.4 %copy-start.1 = (bf16[256,256]{1,0:T(8,128)(2,1)S(1)}, bf16[256,256]{1,0:T(8,128)(2,1)}, u32[]{:S(2)}) copy-start(bf16[256,256]{1,0:T(8,128)(2,1)} %param.8) | copy-start | bytes 393220
Sparse Core Ops, SparseCore 0:
  191.9 150.4 all-reduce.1
where the time goes:
time: 370 us; the launch traced here: 369 us
  waiting for transfers between devices  125 us (34%)
  blocking collectives  100 us (27%)
  matrix products  54.6 us (15%)
  local copies, waits for them, and re-layouts  40.7 us (11%)
  starting transfers between devices  34.1 us (9%)
  between operations  14.1 us (4%)
    psum x1, blocking collectives, local(): conv_grad, gate_grad = lax.psum((conv_part, gate_part), 'ctx')  100 us
    all_to_all x1, waiting for transfers between devices, local(): lax.all_to_all(back_first, 'ctx', split_axis=0, concat_axis=1, tiled=True)  73.7 us
    psum x1, waiting for transfers between devices, local(): conv_grad, gate_grad = lax.psum((conv_part, gate_part), 'ctx')  51.3 us
    all_to_all x1, starting transfers between devices, local(): lax.all_to_all(first, 'ctx', split_axis=1, concat_axis=0, tiled=True)  20.1 us
    dot_general x1, matrix products, local(): gate = jnp.dot(tokens, gate_weight, preferred_element_type=jnp.float32)  17.3 us
    dot_general x1, local copies, waits for them, and re-layouts, local(): jnp.einsum('rdc,rdk->rck', row_factor, lax.all_to_all(back_first, 'ctx',...  9.26 us
    dot_general x1, matrix products, local(): jnp.einsum('rdc,rck->rdk', row_factor, gated, preferred_element_type=jnp....  9.06 us
    dot_general x1, matrix products, local(): jnp.einsum('rdc,rdk->rck', row_factor, lax.all_to_all(back_first, 'ctx',...  8.98 us
  transfers between devices with their start and end apart: 5, of which 2 were waited for; matrix products, arithmetic and copies ran while one was open for 8% of the time, Pallas kernels for 0%

commit v1 on v0

v1 whole, which is shorter than its diff:
```python
import functools

import jax
import jax.numpy as jnp
from jax import lax
from jax.experimental import pallas as pl
from jax.experimental.pallas import tpu as pltpu
from jax.sharding import PartitionSpec as P

F32 = jnp.float32
BF16 = jnp.bfloat16
LANES = 128
GROUP = 4
BACK_SHARES = (1,)
FORWARD_SHARES = (1,)
VMEM_LIMIT = 60 * 1024 * 1024


def params():
    return pltpu.CompilerParams(vmem_limit_bytes=VMEM_LIMIT)


def cost(flops, moved):
    return pl.CostEstimate(flops=flops, bytes_accessed=moved, transcendentals=0)


def contract_first(lhs, rhs):
    return lax.dot_general(lhs, rhs, (((0,), (0,)), ((), ())), preferred_element_type=F32)


def back_first_kernel(peers, col_ref, cot_ref, out_ref):
    runs = out_ref.shape[2]
    for i in range(col_ref.shape[0]):
        value = contract_first(col_ref[i], cot_ref[i]).astype(BF16)
        out_ref[:, i] = value.reshape(peers, runs, value.shape[1])


def back_first_part(peers, col, cot, start, count, group):
    _, order, runs_all = col.shape
    width = cot.shape[2]
    runs = runs_all // peers
    base = start // group
    return pl.pallas_call(
        functools.partial(back_first_kernel, peers),
        grid=(count // group,),
        in_specs=[
            pl.BlockSpec((group, order, runs_all), lambda i: (base + i, 0, 0)),
            pl.BlockSpec((group, order, width), lambda i: (base + i, 0, 0)),
        ],
        out_specs=pl.BlockSpec((peers, group, runs, width), lambda i: (0, i, 0, 0)),
        out_shape=jax.ShapeDtypeStruct((peers, count, runs, width), BF16),
        compiler_params=params(),
        cost_estimate=cost(
            2 * count * order * runs_all * width, 2 * count * (order * runs_all + 2 * order * width)
        ),
    )(col, cot)


def mixed_kernel(peers, col_ref, recv_ref, *refs):
    out_ref = refs[-1]
    for i in range(col_ref.shape[0]):
        first = recv_ref[:, i]
        first = first.reshape(first.shape[0] * first.shape[1], first.shape[2])
        out_ref[i] = jnp.dot(col_ref[i], first, preferred_element_type=F32).astype(BF16)


def mixed_part(peers, col, recv, start, group, before):
    offsets, order, runs_all = col.shape
    count, runs, width = recv.shape[1:]
    base = start // group
    in_specs = [
        pl.BlockSpec((group, order, runs_all), lambda i: (base + i, 0, 0)),
        pl.BlockSpec((peers, group, runs, width), lambda i: (0, i, 0, 0)),
    ]
    operands = [col, recv]
    aliases = {}
    if before is not None:
        in_specs.append(pl.BlockSpec(memory_space=pl.ANY))
        operands.append(before)
        aliases = {2: 0}
    return pl.pallas_call(
        functools.partial(mixed_kernel, peers),
        grid=(count // group,),
        in_specs=in_specs,
        out_specs=pl.BlockSpec((group, order, width), lambda i: (base + i, 0, 0)),
        out_shape=jax.ShapeDtypeStruct((offsets, order, width), BF16),
        input_output_aliases=aliases,
        compiler_params=params(),
        cost_estimate=cost(
            2 * count * order * runs_all * width, 2 * count * (order * runs_all + 2 * order * width)
        ),
    )(*operands)


def shifted(tokens, before, after):
    count = tokens.shape[0]
    at = lax.broadcasted_iota(jnp.int32, tokens.shape, 0)
    low = jnp.where(at == 0, before, pltpu.roll(tokens, 1, 0))
    high = jnp.where(at == count - 1, after, pltpu.roll(tokens, count - 1, 0))
    return low, high


def conv_and_sig(tokens_ref, ends_ref, taps_ref, weight_ref):
    raw = tokens_ref[0]
    tokens = raw.astype(F32)
    low, high = shifted(tokens, ends_ref[0, 0:1], ends_ref[0, 1:2])
    conv = taps_ref[0:1] * low + taps_ref[1:2] * tokens + taps_ref[2:3] * high
    sig = jax.nn.sigmoid(jnp.dot(raw, weight_ref[...], preferred_element_type=F32))
    return raw, tokens, low, high, conv, sig


def first_kernel(peers, starts, tokens_ref, ends_ref, taps_ref, weight_ref, row_ref, *refs):
    outs, held = refs[:-1], refs[-1]
    run = pl.program_id(0)
    runs = pl.num_programs(0)
    count = tokens_ref.shape[1]
    n_runs = outs[0].shape[2]
    _, _, _, _, conv, sig = conv_and_sig(tokens_ref, ends_ref, taps_ref, weight_ref)
    gated = (conv * sig).astype(BF16)
    value = jnp.dot(row_ref[0], gated, preferred_element_type=F32)
    for lane in range(held.shape[0]):
        held[lane, pl.ds(run, count, stride=n_runs), :] = value[:, lane * LANES : (lane + 1) * LANES]

    @pl.when(run == runs - 1)
    def _():
        per_peer = count // peers
        for out, start in zip(outs, starts):
            rows = out.shape[1] * n_runs
            for peer in range(peers):
                at = (peer * per_peer + start) * n_runs
                for lane in range(held.shape[0]):
                    value = held[lane, pl.ds(at, rows), :].astype(BF16)
                    out[peer, :, :, lane * LANES : (lane + 1) * LANES] = value.reshape(out.shape[1], n_runs, LANES)


def first_parts(peers, tokens, ends, taps, weight, row, counts):
    runs, length, width = tokens.shape
    starts = [sum(counts[:i]) for i in range(len(counts))]
    return pl.pallas_call(
        functools.partial(first_kernel, peers, starts),
        grid=(runs,),
        in_specs=[
            pl.BlockSpec((1, length, width), lambda r: (r, 0, 0)),
            pl.BlockSpec((1, 2, width), lambda r: (r, 0, 0)),
            pl.BlockSpec(taps.shape, lambda r: (0, 0)),
            pl.BlockSpec(weight.shape, lambda r: (0, 0)),
            pl.BlockSpec((1, length, length), lambda r: (r, 0, 0)),
        ],
        out_specs=[pl.BlockSpec((peers, c, runs, width), lambda r: (0, 0, 0, 0)) for c in counts],
        out_shape=[jax.ShapeDtypeStruct((peers, c, runs, width), BF16) for c in counts],
        scratch_shapes=[pltpu.VMEM((width // LANES, length * runs, LANES), F32)],
        compiler_params=params(),
        cost_estimate=cost(
            2 * runs * length * width * (length + width), 2 * runs * length * (length + 2 * width)
        ),
    )(tokens, ends, taps, weight, row)


def gradient_kernel(starts, tokens_ref, ends_ref, taps_ref, weight_ref, row_ref, *refs):
    parts, (gate_ref, taps_grad_ref, held) = refs[:-3], refs[-3:]
    run = pl.program_id(0)
    count = tokens_ref.shape[1]
    peers, _, n_runs, width = parts[0].shape
    per_peer = count // peers

    @pl.when(run == 0)
    def _():
        gate_ref[...] = jnp.zeros_like(gate_ref)
        taps_grad_ref[...] = jnp.zeros_like(taps_grad_ref)
        for part, start in zip(parts, starts):
            rows = part.shape[1] * n_runs
            for peer in range(peers):
                at = (peer * per_peer + start) * n_runs
                for lane in range(held.shape[0]):
                    value = part[peer, :, :, lane * LANES : (lane + 1) * LANES]
                    held[lane, pl.ds(at, rows), :] = value.reshape(rows, LANES).astype(F32)

    raw, tokens, low, high, conv, sig = conv_and_sig(tokens_ref, ends_ref, taps_ref, weight_ref)
    back_first = jnp.concatenate(
        [held[lane, pl.ds(run, count, stride=n_runs), :].astype(BF16) for lane in range(held.shape[0])], axis=1
    )
    back_conv = contract_first(row_ref[0], back_first) * sig
    for j, value in enumerate((low, tokens, high)):
        taps_grad_ref[j : j + 1] += jnp.sum(back_conv * value, axis=0, keepdims=True)
    back_gate = (back_conv * conv * (1.0 - sig)).astype(BF16)
    gate_ref[...] += contract_first(raw, back_gate)


def gradient_share(tokens, ends, taps, weight, row, parts):
    runs, length, width = tokens.shape
    counts = [part.shape[1] for part in parts]
    starts = [sum(counts[:i]) for i in range(len(counts))]
    return pl.pallas_call(
        functools.partial(gradient_kernel, starts),
        grid=(runs,),
        in_specs=[
            pl.BlockSpec((1, length, width), lambda r: (r, 0, 0)),
            pl.BlockSpec((1, 2, width), lambda r: (r, 0, 0)),
            pl.BlockSpec(taps.shape, lambda r: (0, 0)),
            pl.BlockSpec(weight.shape, lambda r: (0, 0)),
            pl.BlockSpec((1, length, length), lambda r: (r, 0, 0)),
        ]
        + [pl.BlockSpec(part.shape, lambda r: (0, 0, 0, 0)) for part in parts],
        out_specs=[
            pl.BlockSpec(weight.shape, lambda r: (0, 0)),
            pl.BlockSpec((8, width), lambda r: (0, 0)),
        ],
        out_shape=[
            jax.ShapeDtypeStruct(weight.shape, F32),
            jax.ShapeDtypeStruct((8, width), F32),
        ],
        scratch_shapes=[pltpu.VMEM((width // LANES, length * runs, LANES), F32)],
        compiler_params=params(),
        cost_estimate=cost(
            2 * runs * length * width * (length + 2 * width),
            2 * runs * length * (length + 2 * width),
        ),
    )(tokens, ends, taps, weight, row, *parts)


def exchange(block):
    return lax.all_to_all(block, "ctx", split_axis=0, concat_axis=0, tiled=True)


def total(value, peers):
    step = 1
    while step < peers:
        value = value + lax.ppermute(value, "ctx", [(i, i ^ step) for i in range(peers)])
        step *= 2
    return value


def shares(count, parts):
    return [count * part // sum(parts) for part in parts]


def local(tokens, conv_taps, gate_weight, row_factor, col_factor, cotangent):
    peers = lax.axis_size("ctx")
    width = tokens.shape[1]
    runs, length, _ = row_factor.shape
    offsets = col_factor.shape[0]
    back_got = []
    start = 0
    for count in shares(offsets, BACK_SHARES):
        block = back_first_part(peers, col_factor, cotangent, start, count, GROUP)
        if back_got:
            block, back_got[-1] = lax.optimization_barrier((block, back_got[-1]))
        back_got.append(exchange(block))
        start += count

    rows = tokens.reshape(runs, length, width)
    up = [(i, i + 1) for i in range(peers - 1)]
    down = [(i + 1, i) for i in range(peers - 1)]
    low = lax.ppermute(rows[-1, -1:], "ctx", up)
    high = lax.ppermute(rows[0, :1], "ctx", down)
    before = jnp.concatenate([low, rows[:-1, -1]], axis=0)
    after = jnp.concatenate([rows[1:, 0], high], axis=0)
    ends = jnp.stack([before, after], axis=1).astype(F32)

    counts = shares(offsets, FORWARD_SHARES)
    sent = first_parts(peers, rows, ends, conv_taps, gate_weight, row_factor, counts)
    sent = list(sent)
    sent[0], back_got[-1] = lax.optimization_barrier((sent[0], back_got[-1]))
    got = [exchange(sent[0])]

    gate_share, taps_share = gradient_share(
        rows, ends, conv_taps, gate_weight, row_factor, back_got
    )
    both = total(jnp.concatenate([gate_share, taps_share], axis=0), peers)

    for block in sent[1:]:
        block, got[-1], both = lax.optimization_barrier((block, got[-1], both))
        got.append(exchange(block))
    n_gate = gate_weight.shape[0]
    gate_grad, conv_grad = both[:n_gate], both[n_gate : n_gate + conv_taps.shape[0]]

    mixed = None
    start = 0
    for block in got:
        mixed = mixed_part(peers, col_factor, block, start, GROUP, mixed)
        start += block.shape[1]
    return (mixed, conv_grad, gate_grad)


def solution(mesh):
    placed = (
        P("ctx", "chan"),
        P(None, "chan"),
        P("chan", None),
        P("ctx", None, None),
        P("ctx", None, None),
        P("ctx", None, "chan"),
    )
    return jax.shard_map(
        local,
        mesh=mesh,
        in_specs=placed,
        out_specs=(P("ctx", None, "chan"), P(None, "chan"), P("chan", None)),
        check_vma=False,
    )
```

time: 370 us -> 251 us (0.68)
  blocking collectives: 100 us -> 0 us
  Pallas kernels: 0 us -> 56.6 us
  matrix products: 54.6 us -> 0 us
  local copies, waits for them, and re-layouts: 40.7 us -> 4.63 us
  starting transfers between devices: 34.1 us -> 66.4 us
  between operations: 14.1 us -> 0.73 us
  waiting for transfers between devices: 125 us -> 121 us
    psum x1 -> x0, blocking collectives: 100 us -> none  [local(): conv_grad, gate_grad = lax.psum((conv_part, gate_part), 'ctx')]
    ppermute x2 -> x6, waiting for transfers between devices: 0.01 us -> 74.4 us  [the longest x4 67.2 us: total(): lax.ppermute(value, 'ctx', [(i, i ^ step) for i in range(peers)])]
    pallas_call x0 -> x4, Pallas kernels: none -> 56.6 us  [the longest x1 20.8 us: gradient_share(): pl.pallas_call(functools.partial(gradient_kernel, starts), grid=(runs,),...]
    dot_general x6 -> x0, matrix products: 54.6 us -> none  [the longest x1 17.3 us: local(): gate = jnp.dot(tokens, gate_weight, preferred_element_type=jnp.float32)]
    psum x1 -> x0, waiting for transfers between devices: 51.3 us -> none  [local(): conv_grad, gate_grad = lax.psum((conv_part, gate_part), 'ctx')]
    all_to_all x2, waiting for transfers between devices: 73.7 us -> 46.2 us  [exchange(): return lax.all_to_all(block, 'ctx', split_axis=0, concat_axis=0, tiled=True)]
    all_to_all x2, starting transfers between devices: 28.6 us -> 47.2 us  [exchange(): return lax.all_to_all(block, 'ctx', split_axis=0, concat_axis=0, tiled=True)]
    convert_element_type x2 -> x0, local copies, waits for them, and re-layouts: 15.8 us -> none  [the longest x1 7.94 us: local(): back_first = jnp.einsum('dqr,dqk->rdk', col_factor, cotangent, preferred_...]
  transfers between devices with their start and end apart: 5 -> 8, of which waited for: 2 -> 6; matrix products, arithmetic and copies ran while one was open for 8% -> 2% of each run, Pallas kernels for 0% -> 16%
where the time goes in v1:
time: 251 us; the launch traced here: 250 us
  waiting for transfers between devices  121 us (48%)
  starting transfers between devices  66.4 us (26%)
  Pallas kernels  56.6 us (23%)
  local copies, waits for them, and re-layouts  4.63 us (2%)
    ppermute x4, waiting for transfers between devices, total(): lax.ppermute(value, 'ctx', [(i, i ^ step) for i in range(peers)])  67.2 us
    all_to_all x2, starting transfers between devices, exchange(): return lax.all_to_all(block, 'ctx', split_axis=0, concat_axis=0, tiled=True)  47.2 us
    all_to_all x2, waiting for transfers between devices, exchange(): return lax.all_to_all(block, 'ctx', split_axis=0, concat_axis=0, tiled=True)  46.2 us
    pallas_call x1, Pallas kernels, gradient_share(): pl.pallas_call(functools.partial(gradient_kernel, starts), grid=(runs,),...  20.8 us
    pallas_call x1, Pallas kernels, first_parts(): pl.pallas_call(functools.partial(first_kernel, peers, starts), grid=(runs...  18.8 us
    ppermute x4, starting transfers between devices, total(): lax.ppermute(value, 'ctx', [(i, i ^ step) for i in range(peers)])  14.1 us
    pallas_call x1, Pallas kernels, back_first_part(): pl.pallas_call(functools.partial(back_first_kernel, peers), grid=(count /...  8.62 us
    pallas_call x1, Pallas kernels, mixed_part(): pl.pallas_call(functools.partial(mixed_kernel, peers), grid=(count // gro...  8.33 us
  transfers between devices with their start and end apart: 8, of which 6 were waited for; matrix products, arithmetic and copies ran while one was open for 2% of the time, Pallas kernels for 16%

profile of v1, /device:TPU:0, one launch (start us, length us, event | category | flops | bytes accessed | tf_op | source)
XLA Modules:
  0.0 249.7 jit_solution(12327832155372705488)
XLA Ops:
  0.6 8.6 %shard_map.86 = bf16[16,32,16,256]{3,2,1,0:T(8,128)(2,1)} custom-call(bf16[32,256,256]{2,1,0:T(8,128)(2,1)} %col_ref.3, bf16[32,256,256]{2,1,0:T(8,128)(2,1)} %cot_ref.1), custom_call_target="tpu_custom_call" | custom-call | flops 1073741824 | bytes 12582912 | tf_op jit(solution)/shard_map/pallas_call | solution.py:43
  9.2 8.4 %all-to-all-start = ((bf16[16,32,16,256]{3,2,1,0:T(8,128)(2,1)}), bf16[16,32,16,256]{3,2,1,0:T(8,128)(2,1)}, u32[]{:S(2)}, u32[]{:S(2)}) async-start(bf16[16,32,16,256]{3,2,1,0:T(8,128)(2,1)} %shard_map.86), calls=%async_computation | async-start | bytes 8388608 | tf_op jit(solution)/shard_map/all_to_all | solution.py:222
  17.6 0.7 slice_bitcast_fusion.1
  18.3 3.8 %collective-permute-start = (bf16[1,256]{1,0:T(2,128)(2,1)S(1)}, bf16[1,256]{1,0:T(2,128)(2,1)S(1)}, u32[]{:S(2)}, u32[]{:S(2)}) collective-permute-start(bf16[1,256]{1,0:T(2,128)(2,1)S(1)} %get-tuple-element.11), channel_id=1, source_target_pairs={{0,2},{2,4},{4,6},{6,8},{8,10},{10,12},{12,14},{14,16},{16,18},{18... | collective-permute-start | bytes 1544 | tf_op jit(solution)/shard_map/ppermute | solution.py:254
  22.1 1.3 collective-permute-start.1
  23.4 0.9 fusion
  24.3 7.3 %collective-permute-done = bf16[1,256]{1,0:T(2,128)(2,1)S(1)} collective-permute-done((bf16[1,256]{1,0:T(2,128)(2,1)S(1)}, bf16[1,256]{1,0:T(2,128)(2,1)S(1)}, u32[]{:S(2)}, u32[]{:S(2)}) %collective-permute-start) | collective-permute-done | bytes 544 | tf_op jit(solution)/shard_map/ppermute | solution.py:254
  31.6 0.0 collective-permute-done.1
  31.6 0.7 maximum_convert_fusion.ends_ref
  32.3 18.8 %shard_map.85 = bf16[16,32,16,256]{3,2,1,0:T(8,128)(2,1)} custom-call(bf16[16,512,256]{2,1,0:T(8,128)(2,1)} %bitcast.17, f32[16,2,256]{2,1,0:T(2,128)} %maximum_convert_fusion.ends_ref, f32[3,256]{1,0:T(4,128)} %taps_ref.3, bf16[256,256]{1,0:T(8,128)(2,1)} %weight_ref.3, bf16[16,512,512]{2,1,0:T(8,128)(2,1)} %row_ref.3), custom_call_target="tpu_custom_call" | custom-call | flops 3221225472 | bytes 16777216 | tf_op jit(solution)/shard_map/pallas_call | solution.py:139
  51.1 46.2 %all-to-all-done.refs_0_ = bf16[16,32,16,256]{3,2,1,0:T(8,128)(2,1)} async-done(((bf16[16,32,16,256]{3,2,1,0:T(8,128)(2,1)}), bf16[16,32,16,256]{3,2,1,0:T(8,128)(2,1)}, u32[]{:S(2)}, u32[]{:S(2)}) %all-to-all-start) | async-done | bytes 4194336 | tf_op jit(solution)/shard_map/all_to_all | solution.py:222
  97.3 38.8 %all-to-all-start.1 = ((bf16[16,32,16,256]{3,2,1,0:T(8,128)(2,1)}), bf16[16,32,16,256]{3,2,1,0:T(8,128)(2,1)}, u32[]{:S(2)}, u32[]{:S(2)}) async-start(bf16[16,32,16,256]{3,2,1,0:T(8,128)(2,1)} %shard_map.85), calls=%async_computation.1 | async-start | bytes 8388608 | tf_op jit(solution)/shard_map/all_to_all | solution.py:222
  136.1 20.8 %shard_map.88 = (f32[256,256]{1,0:T(8,128)}, f32[8,256]{1,0:T(8,128)}) custom-call(bf16[16,512,256]{2,1,0:T(8,128)(2,1)} %bitcast.18, f32[16,2,256]{2,1,0:T(2,128)} %maximum_convert_fusion.ends_ref, f32[3,256]{1,0:T(4,128)} %taps_ref.3, bf16[256,256]{1,0:T(8,128)(2,1)} %weight_ref.3, bf16[16,512,512]{2,1,0:T(8,128)(2,1)} %row_ref.3, ...), custom_call_target="tpu_custom_call" | custom-call | flops 4294967296 | bytes 16777216 | tf_op jit(solution)/shard_map/pallas_call | solution.py:193
  156.9 1.0 constant_dynamic-update-slice_fusion.1
  157.9 0.7 constant_dynamic-update-slice_fusion
  158.6 1.9 collective-permute-start.2
  160.5 5.7 %collective-permute-done.2 = f32[264,256]{1,0:T(8,128)S(1)} collective-permute-done((f32[264,256]{1,0:T(8,128)S(1)}, f32[264,256]{1,0:T(8,128)S(1)}, u32[]{:S(2)}, u32[]{:S(2)}) %collective-permute-start.2) | collective-permute-done | bytes 270368 | tf_op jit(solution)/shard_map/ppermute | solution.py:228
  166.2 1.3 collective-permute-start.3
  167.4 11.1 %collective-permute-done.3 = f32[264,256]{1,0:T(8,128)S(1)} collective-permute-done((f32[264,256]{1,0:T(8,128)S(1)}, f32[264,256]{1,0:T(8,128)S(1)}, u32[]{:S(2)}, u32[]{:S(2)}) %collective-permute-start.3) | collective-permute-done | bytes 270368 | tf_op jit(solution)/shard_map/ppermute | solution.py:228
  178.6 5.5 %collective-permute-start.4 = (f32[264,256]{1,0:T(8,128)S(1)}, f32[264,256]{1,0:T(8,128)S(1)}, u32[]{:S(2)}, u32[]{:S(2)}) collective-permute-start(f32[264,256]{1,0:T(8,128)S(1)} %add.13), channel_id=1, source_target_pairs={{0,8},{2,10},{4,12},{6,14},{8,0},{10,2},{12,4},{14,6},{16,24},{18,... | collective-permute-start | bytes 811016 | tf_op jit(solution)/shard_map/ppermute | solution.py:228
  184.1 23.9 %collective-permute-done.4 = f32[264,256]{1,0:T(8,128)S(1)} collective-permute-done((f32[264,256]{1,0:T(8,128)S(1)}, f32[264,256]{1,0:T(8,128)S(1)}, u32[]{:S(2)}, u32[]{:S(2)}) %collective-permute-start.4) | collective-permute-done | bytes 270368 | tf_op jit(solution)/shard_map/ppermute | solution.py:228
  208.0 5.5 %collective-permute-start.5 = (f32[264,256]{1,0:T(8,128)S(1)}, f32[264,256]{1,0:T(8,128)S(1)}, u32[]{:S(2)}, u32[]{:S(2)}) collective-permute-start(f32[264,256]{1,0:T(8,128)S(1)} %add.14), channel_id=1, source_target_pairs={{0,16},{2,18},{4,20},{6,22},{8,24},{10,26},{12,28},{14,30},{16,0},... | collective-permute-start | bytes 811016 | tf_op jit(solution)/shard_map/ppermute | solution.py:228
  213.5 26.5 %collective-permute-done.5 = f32[264,256]{1,0:T(8,128)S(1)} collective-permute-done((f32[264,256]{1,0:T(8,128)S(1)}, f32[264,256]{1,0:T(8,128)S(1)}, u32[]{:S(2)}, u32[]{:S(2)}) %collective-permute-start.5) | collective-permute-done | bytes 270368 | tf_op jit(solution)/shard_map/ppermute | solution.py:228
  240.1 0.6 slice.28
  240.7 0.7 slice.29
  241.4 0.0 all-to-all-done.1.recv_ref
  241.4 8.3 %shard_map.87 = bf16[32,256,256]{2,1,0:T(8,128)(2,1)} custom-call(bf16[32,256,256]{2,1,0:T(8,128)(2,1)} %col_ref.3, bf16[16,32,16,256]{3,2,1,0:T(8,128)(2,1)} %all-to-all-done.1.recv_ref), custom_call_target="tpu_custom_call" | custom-call | flops 1073741824 | bytes 12582912 | tf_op jit(solution)/shard_map/pallas_call | solution.py:81
  (10 shorter events, 0.2 us)
Async XLA Ops:
  9.2 88.1 %all-to-all-start = ((bf16[16,32,16,256]{3,2,1,0:T(8,128)(2,1)}), bf16[16,32,16,256]{3,2,1,0:T(8,128)(2,1)}, u32[]{:S(2)}, u32[]{:S(2)}) async-start(bf16[16,32,16,256]{3,2,1,0:T(8,128)(2,1)} %shard_map.86), calls=%async_computation | async-start | bytes 8388608 | tf_op jit(solution)/shard_map/all_to_all | solution.py:222
  18.3 13.2 %collective-permute-start = (bf16[1,256]{1,0:T(2,128)(2,1)S(1)}, bf16[1,256]{1,0:T(2,128)(2,1)S(1)}, u32[]{:S(2)}, u32[]{:S(2)}) collective-permute-start(bf16[1,256]{1,0:T(2,128)(2,1)S(1)} %get-tuple-element.11), channel_id=1, source_target_pairs={{0,2},{2,4},{4,6},{6,8},{8,10},{10,12},{12,14},{14,16},{16,18},{18... | collective-permute-start | bytes 1544 | tf_op jit(solution)/shard_map/ppermute | solution.py:254
  22.1 9.5 %collective-permute-start.1 = (bf16[1,256]{1,0:T(2,128)(2,1)S(1)}, bf16[1,256]{1,0:T(2,128)(2,1)S(1)}, u32[]{:S(2)}, u32[]{:S(2)}) collective-permute-start(bf16[1,256]{1,0:T(2,128)(2,1)S(1)} %get-tuple-element.12), channel_id=1, source_target_pairs={{2,0},{4,2},{6,4},{8,6},{10,8},{12,10},{14,12},{16,14},{18,16},{20... | collective-permute-start | bytes 1544 | tf_op jit(solution)/shard_map/ppermute | solution.py:255
  97.3 144.0 %all-to-all-start.1 = ((bf16[16,32,16,256]{3,2,1,0:T(8,128)(2,1)}), bf16[16,32,16,256]{3,2,1,0:T(8,128)(2,1)}, u32[]{:S(2)}, u32[]{:S(2)}) async-start(bf16[16,32,16,256]{3,2,1,0:T(8,128)(2,1)} %shard_map.85), calls=%async_computation.1 | async-start | bytes 8388608 | tf_op jit(solution)/shard_map/all_to_all | solution.py:222
  158.6 7.5 %collective-permute-start.2 = (f32[264,256]{1,0:T(8,128)S(1)}, f32[264,256]{1,0:T(8,128)S(1)}, u32[]{:S(2)}, u32[]{:S(2)}) collective-permute-start(f32[264,256]{1,0:T(8,128)S(1)} %constant_dynamic-update-slice_fusion), channel_id=1, source_target_pairs={{0,2},{2,0},{4,6},{6,4},{8,10},{10,8},{12,14},{14,12},{16,18},{18,... | collective-permute-start | bytes 811016 | tf_op jit(solution)/shard_map/ppermute | solution.py:228
  166.2 12.4 %collective-permute-start.3 = (f32[264,256]{1,0:T(8,128)S(1)}, f32[264,256]{1,0:T(8,128)S(1)}, u32[]{:S(2)}, u32[]{:S(2)}) collective-permute-start(f32[264,256]{1,0:T(8,128)S(1)} %add.12), channel_id=1, source_target_pairs={{0,4},{2,6},{4,0},{6,2},{8,12},{10,14},{12,8},{14,10},{16,20},{18,... | collective-permute-start | bytes 811016 | tf_op jit(solution)/shard_map/ppermute | solution.py:228
  178.6 29.4 %collective-permute-start.4 = (f32[264,256]{1,0:T(8,128)S(1)}, f32[264,256]{1,0:T(8,128)S(1)}, u32[]{:S(2)}, u32[]{:S(2)}) collective-permute-start(f32[264,256]{1,0:T(8,128)S(1)} %add.13), channel_id=1, source_target_pairs={{0,8},{2,10},{4,12},{6,14},{8,0},{10,2},{12,4},{14,6},{16,24},{18,... | collective-permute-start | bytes 811016 | tf_op jit(solution)/shard_map/ppermute | solution.py:228
  208.0 32.0 %collective-permute-start.5 = (f32[264,256]{1,0:T(8,128)S(1)}, f32[264,256]{1,0:T(8,128)S(1)}, u32[]{:S(2)}, u32[]{:S(2)}) collective-permute-start(f32[264,256]{1,0:T(8,128)S(1)} %add.14), channel_id=1, source_target_pairs={{0,16},{2,18},{4,20},{6,22},{8,24},{10,26},{12,28},{14,30},{16,0},... | collective-permute-start | bytes 811016 | tf_op jit(solution)/shard_map/ppermute | solution.py:228

commit v2 on v1

--- a/solution.py
+++ b/solution.py
@@ -11,8 +11,6 @@
 BF16 = jnp.bfloat16
 LANES = 128
 GROUP = 4
-BACK_SHARES = (1,)
-FORWARD_SHARES = (1,)
 VMEM_LIMIT = 60 * 1024 * 1024
 
 
@@ -28,68 +26,101 @@
     return lax.dot_general(lhs, rhs, (((0,), (0,)), ((), ())), preferred_element_type=F32)
 
 
-def back_first_kernel(peers, col_ref, cot_ref, out_ref):
-    runs = out_ref.shape[2]
-    for i in range(col_ref.shape[0]):
-        value = contract_first(col_ref[i], cot_ref[i]).astype(BF16)
-        out_ref[:, i] = value.reshape(peers, runs, value.shape[1])
-
-
-def back_first_part(peers, col, cot, start, count, group):
-    _, order, runs_all = col.shape
+def copies(pairs, sems, at):
+    return [pltpu.make_async_copy(source, target, sems.at[at + i]) for i, (source, target) in enumerate(pairs)]
+
+
+def back_first_kernel(peers, group, col, cot, out, col_held, cot_held, out_held, in_sems, out_sems):
+    offsets, _, width = cot_held.shape
+    runs = out_held.shape[2]
+    steps = [pl.ds(start, group) for start in range(0, offsets, group)]
+    loads = [
+        copies([(col.at[at], col_held.at[at]), (cot.at[at], cot_held.at[at])], in_sems, 2 * i)
+        for i, at in enumerate(steps)
+    ]
+    stores = [copies([(out_held.at[:, at], out.at[:, at])], out_sems, i) for i, at in enumerate(steps)]
+    for load in loads:
+        for copy in load:
+            copy.start()
+    for i, at in enumerate(steps):
+        for copy in loads[i]:
+            copy.wait()
+        for d in range(i * group, (i + 1) * group):
+            value = contract_first(col_held[d], cot_held[d]).astype(BF16)
+            out_held[:, d] = value.reshape(peers, runs, width)
+        stores[i][0].start()
+    for store in stores:
+        store[0].wait()
+
+
+def back_first_all(peers, col, cot):
+    offsets, order, runs_all = col.shape
     width = cot.shape[2]
-    runs = runs_all // peers
-    base = start // group
+    shape = (peers, offsets, runs_all // peers, width)
+    steps = offsets // GROUP
     return pl.pallas_call(
-        functools.partial(back_first_kernel, peers),
-        grid=(count // group,),
-        in_specs=[
-            pl.BlockSpec((group, order, runs_all), lambda i: (base + i, 0, 0)),
-            pl.BlockSpec((group, order, width), lambda i: (base + i, 0, 0)),
-        ],
-        out_specs=pl.BlockSpec((peers, group, runs, width), lambda i: (0, i, 0, 0)),
-        out_shape=jax.ShapeDtypeStruct((peers, count, runs, width), BF16),
+        functools.partial(back_first_kernel, peers, GROUP),
+        in_specs=[pl.BlockSpec(memory_space=pl.ANY)] * 2,
+        out_specs=pl.BlockSpec(memory_space=pl.ANY),
+        out_shape=jax.ShapeDtypeStruct(shape, BF16),
+        scratch_shapes=[
+            pltpu.VMEM(col.shape, BF16),
+            pltpu.VMEM(cot.shape, BF16),
+            pltpu.VMEM(shape, BF16),
+            pltpu.SemaphoreType.DMA((2 * steps,)),
+            pltpu.SemaphoreType.DMA((steps,)),
+        ],
         compiler_params=params(),
         cost_estimate=cost(
-            2 * count * order * runs_all * width, 2 * count * (order * runs_all + 2 * order * width)
+            2 * offsets * order * runs_all * width, 2 * offsets * (order * runs_all + 2 * order * width)
         ),
     )(col, cot)
 
 
-def mixed_kernel(peers, col_ref, recv_ref, *refs):
-    out_ref = refs[-1]
-    for i in range(col_ref.shape[0]):
-        first = recv_ref[:, i]
-        first = first.reshape(first.shape[0] * first.shape[1], first.shape[2])
-        out_ref[i] = jnp.dot(col_ref[i], first, preferred_element_type=F32).astype(BF16)
-
-
-def mixed_part(peers, col, recv, start, group, before):
+def mixed_kernel(group, col, recv, out, col_held, recv_held, out_held, in_sems, out_sems):
+    peers, offsets, runs, width = recv_held.shape
+    steps = [pl.ds(start, group) for start in range(0, offsets, group)]
+    loads = [
+        copies([(col.at[at], col_held.at[at]), (recv.at[:, at], recv_held.at[:, at])], in_sems, 2 * i)
+        for i, at in enumerate(steps)
+    ]
+    stores = [copies([(out_held.at[at], out.at[at])], out_sems, i) for i, at in enumerate(steps)]
+    for load in loads:
+        for copy in load:
+            copy.start()
+    for i, at in enumerate(steps):
+        for copy in loads[i]:
+            copy.wait()
+        for d in range(i * group, (i + 1) * group):
+            first = recv_held[:, d].reshape(peers * runs, width)
+            out_held[d] = jnp.dot(col_held[d], first, preferred_element_type=F32).astype(BF16)
+        stores[i][0].start()
+    for store in stores:
+        store[0].wait()
+
+
+def mixed_all(col, recv):
     offsets, order, runs_all = col.shape
-    count, runs, width = recv.shape[1:]
-    base = start // group
-    in_specs = [
-        pl.BlockSpec((group, order, runs_all), lambda i: (base + i, 0, 0)),
-        pl.BlockSpec((peers, group, runs, width), lambda i: (0, i, 0, 0)),
-    ]
-    operands = [col, recv]
-    aliases = {}
-    if before is not None:
-        in_specs.append(pl.BlockSpec(memory_space=pl.ANY))
-        operands.append(before)
-        aliases = {2: 0}
+    width = recv.shape[3]
+    shape = (offsets, order, width)
+    steps = offsets // GROUP
     return pl.pallas_call(
-        functools.partial(mixed_kernel, peers),
-        grid=(count // group,),
-        in_specs=in_specs,
-        out_specs=pl.BlockSpec((group, order, width), lambda i: (base + i, 0, 0)),
-        out_shape=jax.ShapeDtypeStruct((offsets, order, width), BF16),
-        input_output_aliases=aliases,
+        functools.partial(mixed_kernel, GROUP),
+        in_specs=[pl.BlockSpec(memory_space=pl.ANY)] * 2,
+        out_specs=pl.BlockSpec(memory_space=pl.ANY),
+        out_shape=jax.ShapeDtypeStruct(shape, BF16),
+        scratch_shapes=[
+            pltpu.VMEM(col.shape, BF16),
+            pltpu.VMEM(recv.shape, BF16),
+            pltpu.VMEM(shape, BF16),
+            pltpu.SemaphoreType.DMA((2 * steps,)),
+            pltpu.SemaphoreType.DMA((steps,)),
+        ],
         compiler_params=params(),
         cost_estimate=cost(
-            2 * count * order * runs_all * width, 2 * count * (order * runs_all + 2 * order * width)
+            2 * offsets * order * runs_all * width, 2 * offsets * (order * runs_all + 2 * order * width)
         ),
-    )(*operands)
+    )(col, recv)
 
 
 def shifted(tokens, before, after):
@@ -230,56 +261,35 @@
     return value
 
 
-def shares(count, parts):
-    return [count * part // sum(parts) for part in parts]
-
-
 def local(tokens, conv_taps, gate_weight, row_factor, col_factor, cotangent):
     peers = lax.axis_size("ctx")
     width = tokens.shape[1]
     runs, length, _ = row_factor.shape
     offsets = col_factor.shape[0]
-    back_got = []
-    start = 0
-    for count in shares(offsets, BACK_SHARES):
-        block = back_first_part(peers, col_factor, cotangent, start, count, GROUP)
-        if back_got:
-            block, back_got[-1] = lax.optimization_barrier((block, back_got[-1]))
-        back_got.append(exchange(block))
-        start += count
-
     rows = tokens.reshape(runs, length, width)
     up = [(i, i + 1) for i in range(peers - 1)]
     down = [(i + 1, i) for i in range(peers - 1)]
-    low = lax.ppermute(rows[-1, -1:], "ctx", up)
-    high = lax.ppermute(rows[0, :1], "ctx", down)
+    low = lax.ppermute(tokens[-1:], "ctx", up)
+    high = lax.ppermute(tokens[:1], "ctx", down)
+
+    block = back_first_all(peers, col_factor, cotangent)
+    block, low, high = lax.optimization_barrier((block, low, high))
+    back_got = exchange(block)
+
     before = jnp.concatenate([low, rows[:-1, -1]], axis=0)
     after = jnp.concatenate([rows[1:, 0], high], axis=0)
     ends = jnp.stack([before, after], axis=1).astype(F32)
-
-    counts = shares(offsets, FORWARD_SHARES)
-    sent = first_parts(peers, rows, ends, conv_taps, gate_weight, row_factor, counts)
-    sent = list(sent)
-    sent[0], back_got[-1] = lax.optimization_barrier((sent[0], back_got[-1]))
-    got = [exchange(sent[0])]
+    (sent,) = first_parts(peers, rows, ends, conv_taps, gate_weight, row_factor, (offsets,))
+    sent, back_got = lax.optimization_barrier((sent, back_got))
+    got = exchange(sent)
 
     gate_share, taps_share = gradient_share(
-        rows, ends, conv_taps, gate_weight, row_factor, back_got
+        rows, ends, conv_taps, gate_weight, row_factor, [back_got]
     )
     both = total(jnp.concatenate([gate_share, taps_share], axis=0), peers)
-
-    for block in sent[1:]:
-        block, got[-1], both = lax.optimization_barrier((block, got[-1], both))
-        got.append(exchange(block))
     n_gate = gate_weight.shape[0]
     gate_grad, conv_grad = both[:n_gate], both[n_gate : n_gate + conv_taps.shape[0]]
-
-    mixed = None
-    start = 0
-    for block in got:
-        mixed = mixed_part(peers, col_factor, block, start, GROUP, mixed)
-        start += block.shape[1]
-    return (mixed, conv_grad, gate_grad)
+    return (mixed_all(col_factor, got), conv_grad, gate_grad)
 
 
 def solution(mesh):

time: 251 us -> 232 us (0.924)
  starting transfers between devices: 66.4 us -> 45.4 us
  waiting for transfers between devices: 121 us -> 129 us
  Pallas kernels: 56.6 us -> 51 us
    all_to_all x2, starting transfers between devices: 47.2 us -> 27.7 us  [exchange(): return lax.all_to_all(block, 'ctx', split_axis=0, concat_axis=0, tiled=True)]
    all_to_all x2, waiting for transfers between devices: 46.2 us -> 58.2 us  [exchange(): return lax.all_to_all(block, 'ctx', split_axis=0, concat_axis=0, tiled=True)]
    ppermute x2, waiting for transfers between devices: 7.26 us -> 0.01 us  [the longest x1 0.01 us: local(): high = lax.ppermute(tokens[:1], 'ctx', down)]
    pallas_call x2, Pallas kernels: 16.9 us -> 11.3 us  [the longest x1 5.7 us: back_first_all(): pl.pallas_call(functools.partial(back_first_kernel, peers, GROUP), in_spe...]
    ppermute x4, waiting for transfers between devices: 67.2 us -> 70.4 us  [total(): lax.ppermute(value, 'ctx', [(i, i ^ step) for i in range(peers)])]
    ppermute x4, starting transfers between devices: 14.1 us -> 11 us  [total(): lax.ppermute(value, 'ctx', [(i, i ^ step) for i in range(peers)])]
  transfers between devices with their start and end apart: 8 -> 8, of which waited for: 6 -> 5; matrix products, arithmetic and copies ran while one was open for 2% -> 2% of each run, Pallas kernels for 16% -> 20%
where the time goes in v2:
time: 232 us; the launch traced here: 231 us
  waiting for transfers between devices  129 us (56%)
  Pallas kernels  51 us (22%)
  starting transfers between devices  45.4 us (20%)
  local copies, waits for them, and re-layouts  4.62 us (2%)
    ppermute x4, waiting for transfers between devices, total(): lax.ppermute(value, 'ctx', [(i, i ^ step) for i in range(peers)])  70.4 us
    all_to_all x2, waiting for transfers between devices, exchange(): return lax.all_to_all(block, 'ctx', split_axis=0, concat_axis=0, tiled=True)  58.2 us
    all_to_all x2, starting transfers between devices, exchange(): return lax.all_to_all(block, 'ctx', split_axis=0, concat_axis=0, tiled=True)  27.7 us
    pallas_call x1, Pallas kernels, gradient_share(): pl.pallas_call(functools.partial(gradient_kernel, starts), grid=(runs,),...  20.8 us
    pallas_call x1, Pallas kernels, first_parts(): pl.pallas_call(functools.partial(first_kernel, peers, starts), grid=(runs...  18.8 us
    ppermute x4, starting transfers between devices, total(): lax.ppermute(value, 'ctx', [(i, i ^ step) for i in range(peers)])  11 us
    pallas_call x1, Pallas kernels, back_first_all(): pl.pallas_call(functools.partial(back_first_kernel, peers, GROUP), in_spe...  5.7 us
    pallas_call x1, Pallas kernels, mixed_all(): pl.pallas_call(functools.partial(mixed_kernel, GROUP), in_specs=[pl.Block...  5.63 us
  transfers between devices with their start and end apart: 8, of which 5 were waited for; matrix products, arithmetic and copies ran while one was open for 2% of the time, Pallas kernels for 20%

profile of v2, /device:TPU:0, one launch (start us, length us, event | category | flops | bytes accessed | tf_op | source)
XLA Modules:
  0.0 231.2 jit_solution(4261602302661020165)
XLA Ops:
  0.6 0.7 fusion.1
  1.3 1.3 collective-permute-start.1
  2.6 5.5 %collective-permute-start = (bf16[1,256]{1,0:T(2,128)(2,1)S(1)}, bf16[1,256]{1,0:T(2,128)(2,1)S(1)}, u32[]{:S(2)}, u32[]{:S(2)}) collective-permute-start(bf16[1,256]{1,0:T(2,128)(2,1)S(1)} %get-tuple-element.20), channel_id=1, source_target_pairs={{0,2},{2,4},{4,6},{6,8},{8,10},{10,12},{12,14},{14,16},{16,18},{18... | collective-permute-start | bytes 1544 | tf_op jit(solution)/shard_map/ppermute | solution.py:272
  8.1 5.7 %shard_map.85 = bf16[16,32,16,256]{3,2,1,0:T(8,128)(2,1)} custom-call(bf16[32,256,256]{2,1,0:T(8,128)(2,1)} %col.3, bf16[32,256,256]{2,1,0:T(8,128)(2,1)} %cot.1), custom_call_target="tpu_custom_call" | custom-call | flops 1073741824 | bytes 12582912 | tf_op jit(solution)/shard_map/pallas_call | solution.py:61
  13.8 0.0 collective-permute-done.1
  13.8 0.0 collective-permute-done
  13.8 8.2 %all-to-all-start = ((bf16[16,32,16,256]{3,2,1,0:T(8,128)(2,1)}), bf16[16,32,16,256]{3,2,1,0:T(8,128)(2,1)}, u32[]{:S(2)}, u32[]{:S(2)}) async-start(bf16[16,32,16,256]{3,2,1,0:T(8,128)(2,1)} %shard_map.85), calls=%async_computation | async-start | bytes 8388608 | tf_op jit(solution)/shard_map/all_to_all | solution.py:253
  22.1 0.9 fusion
  23.1 0.6 maximum_convert_fusion.ends_ref
  23.7 18.8 %shard_map.86 = bf16[16,32,16,256]{3,2,1,0:T(8,128)(2,1)} custom-call(bf16[16,512,256]{2,1,0:T(8,128)(2,1)} %bitcast.12, f32[16,2,256]{2,1,0:T(2,128)} %maximum_convert_fusion.ends_ref, f32[3,256]{1,0:T(4,128)} %taps_ref.3, bf16[256,256]{1,0:T(8,128)(2,1)} %weight_ref.3, bf16[16,512,512]{2,1,0:T(8,128)(2,1)} %row_ref.3), custom_call_target="tpu_custom_call" | custom-call | flops 3221225472 | bytes 16777216 | tf_op jit(solution)/shard_map/pallas_call | solution.py:170
  42.6 58.2 %all-to-all-done.refs_0_ = bf16[16,32,16,256]{3,2,1,0:T(8,128)(2,1)} async-done(((bf16[16,32,16,256]{3,2,1,0:T(8,128)(2,1)}), bf16[16,32,16,256]{3,2,1,0:T(8,128)(2,1)}, u32[]{:S(2)}, u32[]{:S(2)}) %all-to-all-start) | async-done | bytes 4194336 | tf_op jit(solution)/shard_map/all_to_all | solution.py:253
  100.8 19.5 %all-to-all-start.1 = ((bf16[16,32,16,256]{3,2,1,0:T(8,128)(2,1)}), bf16[16,32,16,256]{3,2,1,0:T(8,128)(2,1)}, u32[]{:S(2)}, u32[]{:S(2)}) async-start(bf16[16,32,16,256]{3,2,1,0:T(8,128)(2,1)} %shard_map.86), calls=%async_computation.1 | async-start | bytes 8388608 | tf_op jit(solution)/shard_map/all_to_all | solution.py:253
  120.3 20.8 %shard_map.88 = (f32[256,256]{1,0:T(8,128)}, f32[8,256]{1,0:T(8,128)}) custom-call(bf16[16,512,256]{2,1,0:T(8,128)(2,1)} %bitcast.13, f32[16,2,256]{2,1,0:T(2,128)} %maximum_convert_fusion.ends_ref, f32[3,256]{1,0:T(4,128)} %taps_ref.3, bf16[256,256]{1,0:T(8,128)(2,1)} %weight_ref.3, bf16[16,512,512]{2,1,0:T(8,128)(2,1)} %row_ref.3, ...), custom_call_target="tpu_custom_call" | custom-call | flops 4294967296 | bytes 16777216 | tf_op jit(solution)/shard_map/pallas_call | solution.py:224
  141.1 1.0 constant_dynamic-update-slice_fusion.1
  142.0 0.7 constant_dynamic-update-slice_fusion
  142.7 1.9 collective-permute-start.2
  144.6 6.4 %collective-permute-done.2 = f32[264,256]{1,0:T(8,128)S(1)} collective-permute-done((f32[264,256]{1,0:T(8,128)S(1)}, f32[264,256]{1,0:T(8,128)S(1)}, u32[]{:S(2)}, u32[]{:S(2)}) %collective-permute-start.2) | collective-permute-done | bytes 270368 | tf_op jit(solution)/shard_map/ppermute | solution.py:259
  151.1 0.6 collective-permute-start.3
  151.7 12.8 %collective-permute-done.3 = f32[264,256]{1,0:T(8,128)S(1)} collective-permute-done((f32[264,256]{1,0:T(8,128)S(1)}, f32[264,256]{1,0:T(8,128)S(1)}, u32[]{:S(2)}, u32[]{:S(2)}) %collective-permute-start.3) | collective-permute-done | bytes 270368 | tf_op jit(solution)/shard_map/ppermute | solution.py:259
  164.5 4.8 %collective-permute-start.4 = (f32[264,256]{1,0:T(8,128)S(1)}, f32[264,256]{1,0:T(8,128)S(1)}, u32[]{:S(2)}, u32[]{:S(2)}) collective-permute-start(f32[264,256]{1,0:T(8,128)S(1)} %add.13), channel_id=1, source_target_pairs={{0,8},{2,10},{4,12},{6,14},{8,0},{10,2},{12,4},{14,6},{16,24},{18,... | collective-permute-start | bytes 811016 | tf_op jit(solution)/shard_map/ppermute | solution.py:259
  169.3 24.5 %collective-permute-done.4 = f32[264,256]{1,0:T(8,128)S(1)} collective-permute-done((f32[264,256]{1,0:T(8,128)S(1)}, f32[264,256]{1,0:T(8,128)S(1)}, u32[]{:S(2)}, u32[]{:S(2)}) %collective-permute-start.4) | collective-permute-done | bytes 270368 | tf_op jit(solution)/shard_map/ppermute | solution.py:259
  193.8 3.7 %collective-permute-start.5 = (f32[264,256]{1,0:T(8,128)S(1)}, f32[264,256]{1,0:T(8,128)S(1)}, u32[]{:S(2)}, u32[]{:S(2)}) collective-permute-start(f32[264,256]{1,0:T(8,128)S(1)} %add.14), channel_id=1, source_target_pairs={{0,16},{2,18},{4,20},{6,22},{8,24},{10,26},{12,28},{14,30},{16,0},... | collective-permute-start | bytes 811016 | tf_op jit(solution)/shard_map/ppermute | solution.py:259
  197.6 26.6 %collective-permute-done.5 = f32[264,256]{1,0:T(8,128)S(1)} collective-permute-done((f32[264,256]{1,0:T(8,128)S(1)}, f32[264,256]{1,0:T(8,128)S(1)}, u32[]{:S(2)}, u32[]{:S(2)}) %collective-permute-start.5) | collective-permute-done | bytes 270368 | tf_op jit(solution)/shard_map/ppermute | solution.py:259
  224.2 0.6 slice.26
  224.8 0.7 slice.27
  225.6 0.0 all-to-all-done.1.recv
  225.6 5.6 %shard_map.87 = bf16[32,256,256]{2,1,0:T(8,128)(2,1)} custom-call(bf16[32,256,256]{2,1,0:T(8,128)(2,1)} %col.3, bf16[16,32,16,256]{3,2,1,0:T(8,128)(2,1)} %all-to-all-done.1.recv), custom_call_target="tpu_custom_call" | custom-call | flops 1073741824 | bytes 12582912 | tf_op jit(solution)/shard_map/pallas_call | solution.py:107
  (9 shorter events, 0.2 us)
Async XLA Ops:
  1.3 12.5 %collective-permute-start.1 = (bf16[1,256]{1,0:T(2,128)(2,1)S(1)}, bf16[1,256]{1,0:T(2,128)(2,1)S(1)}, u32[]{:S(2)}, u32[]{:S(2)}) collective-permute-start(bf16[1,256]{1,0:T(2,128)(2,1)S(1)} %get-tuple-element.19), channel_id=1, source_target_pairs={{2,0},{4,2},{6,4},{8,6},{10,8},{12,10},{14,12},{16,14},{18,16},{20... | collective-permute-start | bytes 1544 | tf_op jit(solution)/shard_map/ppermute | solution.py:273
  2.6 11.2 %collective-permute-start = (bf16[1,256]{1,0:T(2,128)(2,1)S(1)}, bf16[1,256]{1,0:T(2,128)(2,1)S(1)}, u32[]{:S(2)}, u32[]{:S(2)}) collective-permute-start(bf16[1,256]{1,0:T(2,128)(2,1)S(1)} %get-tuple-element.20), channel_id=1, source_target_pairs={{0,2},{2,4},{4,6},{6,8},{8,10},{10,12},{12,14},{14,16},{16,18},{18... | collective-permute-start | bytes 1544 | tf_op jit(solution)/shard_map/ppermute | solution.py:272
  13.8 86.9 %all-to-all-start = ((bf16[16,32,16,256]{3,2,1,0:T(8,128)(2,1)}), bf16[16,32,16,256]{3,2,1,0:T(8,128)(2,1)}, u32[]{:S(2)}, u32[]{:S(2)}) async-start(bf16[16,32,16,256]{3,2,1,0:T(8,128)(2,1)} %shard_map.85), calls=%async_computation | async-start | bytes 8388608 | tf_op jit(solution)/shard_map/all_to_all | solution.py:253
  100.8 124.8 %all-to-all-start.1 = ((bf16[16,32,16,256]{3,2,1,0:T(8,128)(2,1)}), bf16[16,32,16,256]{3,2,1,0:T(8,128)(2,1)}, u32[]{:S(2)}, u32[]{:S(2)}) async-start(bf16[16,32,16,256]{3,2,1,0:T(8,128)(2,1)} %shard_map.86), calls=%async_computation.1 | async-start | bytes 8388608 | tf_op jit(solution)/shard_map/all_to_all | solution.py:253
  142.7 8.3 %collective-permute-start.2 = (f32[264,256]{1,0:T(8,128)S(1)}, f32[264,256]{1,0:T(8,128)S(1)}, u32[]{:S(2)}, u32[]{:S(2)}) collective-permute-start(f32[264,256]{1,0:T(8,128)S(1)} %constant_dynamic-update-slice_fusion), channel_id=1, source_target_pairs={{0,2},{2,0},{4,6},{6,4},{8,10},{10,8},{12,14},{14,12},{16,18},{18,... | collective-permute-start | bytes 811016 | tf_op jit(solution)/shard_map/ppermute | solution.py:259
  151.1 13.4 %collective-permute-start.3 = (f32[264,256]{1,0:T(8,128)S(1)}, f32[264,256]{1,0:T(8,128)S(1)}, u32[]{:S(2)}, u32[]{:S(2)}) collective-permute-start(f32[264,256]{1,0:T(8,128)S(1)} %add.12), channel_id=1, source_target_pairs={{0,4},{2,6},{4,0},{6,2},{8,12},{10,14},{12,8},{14,10},{16,20},{18,... | collective-permute-start | bytes 811016 | tf_op jit(solution)/shard_map/ppermute | solution.py:259
  164.5 29.3 %collective-permute-start.4 = (f32[264,256]{1,0:T(8,128)S(1)}, f32[264,256]{1,0:T(8,128)S(1)}, u32[]{:S(2)}, u32[]{:S(2)}) collective-permute-start(f32[264,256]{1,0:T(8,128)S(1)} %add.13), channel_id=1, source_target_pairs={{0,8},{2,10},{4,12},{6,14},{8,0},{10,2},{12,4},{14,6},{16,24},{18,... | collective-permute-start | bytes 811016 | tf_op jit(solution)/shard_map/ppermute | solution.py:259
  193.8 30.4 %collective-permute-start.5 = (f32[264,256]{1,0:T(8,128)S(1)}, f32[264,256]{1,0:T(8,128)S(1)}, u32[]{:S(2)}, u32[]{:S(2)}) collective-permute-start(f32[264,256]{1,0:T(8,128)S(1)} %add.14), channel_id=1, source_target_pairs={{0,16},{2,18},{4,20},{6,22},{8,24},{10,26},{12,28},{14,30},{16,0},... | collective-permute-start | bytes 811016 | tf_op jit(solution)/shard_map/ppermute | solution.py:259

commit v3 on v2

--- a/solution.py
+++ b/solution.py
@@ -11,6 +11,10 @@
 BF16 = jnp.bfloat16
 LANES = 128
 GROUP = 4
+QUARTERS = 4
+PAD = 8
+BACK_PARTS = (1, 3)
+FORWARD_PARTS = (3, 1)
 VMEM_LIMIT = 60 * 1024 * 1024
 
 
@@ -30,12 +34,19 @@
     return [pltpu.make_async_copy(source, target, sems.at[at + i]) for i, (source, target) in enumerate(pairs)]
 
 
-def back_first_kernel(peers, group, col, cot, out, col_held, cot_held, out_held, in_sems, out_sems):
+def back_first_kernel(peers, group, first, col, cot, out, col_held, cot_held, out_held, in_sems, out_sems):
     offsets, _, width = cot_held.shape
     runs = out_held.shape[2]
     steps = [pl.ds(start, group) for start in range(0, offsets, group)]
     loads = [
-        copies([(col.at[at], col_held.at[at]), (cot.at[at], cot_held.at[at])], in_sems, 2 * i)
+        copies(
+            [
+                (col.at[pl.ds(first + i * group, group)], col_held.at[at]),
+                (cot.at[pl.ds(first + i * group, group)], cot_held.at[at]),
+            ],
+            in_sems,
+            2 * i,
+        )
         for i, at in enumerate(steps)
     ]
     stores = [copies([(out_held.at[:, at], out.at[:, at])], out_sems, i) for i, at in enumerate(steps)]
@@ -53,74 +64,79 @@
         store[0].wait()
 
 
-def back_first_all(peers, col, cot):
-    offsets, order, runs_all = col.shape
+def back_first_part(peers, col, cot, start, count):
+    _, order, runs_all = col.shape
     width = cot.shape[2]
-    shape = (peers, offsets, runs_all // peers, width)
-    steps = offsets // GROUP
+    shape = (peers, count, runs_all // peers, width)
+    steps = count // GROUP
     return pl.pallas_call(
-        functools.partial(back_first_kernel, peers, GROUP),
+        functools.partial(back_first_kernel, peers, GROUP, start),
         in_specs=[pl.BlockSpec(memory_space=pl.ANY)] * 2,
         out_specs=pl.BlockSpec(memory_space=pl.ANY),
         out_shape=jax.ShapeDtypeStruct(shape, BF16),
         scratch_shapes=[
-            pltpu.VMEM(col.shape, BF16),
-            pltpu.VMEM(cot.shape, BF16),
+            pltpu.VMEM((count, order, runs_all), BF16),
+            pltpu.VMEM((count, order, width), BF16),
             pltpu.VMEM(shape, BF16),
             pltpu.SemaphoreType.DMA((2 * steps,)),
             pltpu.SemaphoreType.DMA((steps,)),
         ],
         compiler_params=params(),
         cost_estimate=cost(
-            2 * offsets * order * runs_all * width, 2 * offsets * (order * runs_all + 2 * order * width)
+            2 * count * order * runs_all * width, 2 * count * (order * runs_all + 2 * order * width)
         ),
     )(col, cot)
 
 
-def mixed_kernel(group, col, recv, out, col_held, recv_held, out_held, in_sems, out_sems):
+def mixed_kernel(group, first, col, recv, *refs):
+    out, col_held, recv_held, out_held, in_sems, out_sems = refs[-6:]
     peers, offsets, runs, width = recv_held.shape
     steps = [pl.ds(start, group) for start in range(0, offsets, group)]
+    rows = [pl.ds(first + start, group) for start in range(0, offsets, group)]
     loads = [
-        copies([(col.at[at], col_held.at[at]), (recv.at[:, at], recv_held.at[:, at])], in_sems, 2 * i)
-        for i, at in enumerate(steps)
+        copies([(col.at[row], col_held.at[at]), (recv.at[:, at], recv_held.at[:, at])], in_sems, 2 * i)
+        for i, (row, at) in enumerate(zip(rows, steps))
     ]
-    stores = [copies([(out_held.at[at], out.at[at])], out_sems, i) for i, at in enumerate(steps)]
+    stores = [
+        copies([(out_held.at[at], out.at[row])], out_sems, i) for i, (row, at) in enumerate(zip(rows, steps))
+    ]
     for load in loads:
         for copy in load:
             copy.start()
-    for i, at in enumerate(steps):
+    for i in range(len(steps)):
         for copy in loads[i]:
             copy.wait()
         for d in range(i * group, (i + 1) * group):
-            first = recv_held[:, d].reshape(peers * runs, width)
-            out_held[d] = jnp.dot(col_held[d], first, preferred_element_type=F32).astype(BF16)
+            value = recv_held[:, d].reshape(peers * runs, width)
+            out_held[d] = jnp.dot(col_held[d], value, preferred_element_type=F32).astype(BF16)
         stores[i][0].start()
     for store in stores:
         store[0].wait()
 
 
-def mixed_all(col, recv):
+def mixed_part(col, recv, start, before):
     offsets, order, runs_all = col.shape
-    width = recv.shape[3]
-    shape = (offsets, order, width)
-    steps = offsets // GROUP
+    count, width = recv.shape[1], recv.shape[3]
+    steps = count // GROUP
+    operands = [col, recv] if before is None else [col, recv, before]
     return pl.pallas_call(
-        functools.partial(mixed_kernel, GROUP),
-        in_specs=[pl.BlockSpec(memory_space=pl.ANY)] * 2,
+        functools.partial(mixed_kernel, GROUP, start),
+        in_specs=[pl.BlockSpec(memory_space=pl.ANY)] * len(operands),
         out_specs=pl.BlockSpec(memory_space=pl.ANY),
-        out_shape=jax.ShapeDtypeStruct(shape, BF16),
+        out_shape=jax.ShapeDtypeStruct((offsets, order, width), BF16),
+        input_output_aliases={} if before is None else {2: 0},
         scratch_shapes=[
-            pltpu.VMEM(col.shape, BF16),
+            pltpu.VMEM((count, order, runs_all), BF16),
             pltpu.VMEM(recv.shape, BF16),
-            pltpu.VMEM(shape, BF16),
+            pltpu.VMEM((count, order, width), BF16),
             pltpu.SemaphoreType.DMA((2 * steps,)),
             pltpu.SemaphoreType.DMA((steps,)),
         ],
         compiler_params=params(),
         cost_estimate=cost(
-            2 * offsets * order * runs_all * width, 2 * offsets * (order * runs_all + 2 * order * width)
+            2 * count * order * runs_all * width, 2 * count * (order * runs_all + 2 * order * width)
         ),
-    )(col, recv)
+    )(*operands)
 
 
 def shifted(tokens, before, after):
@@ -188,23 +204,23 @@
 
 
 def gradient_kernel(starts, tokens_ref, ends_ref, taps_ref, weight_ref, row_ref, *refs):
-    parts, (gate_ref, taps_grad_ref, held) = refs[:-3], refs[-3:]
+    parts, (share_ref, held) = refs[:-2], refs[-2:]
     run = pl.program_id(0)
     count = tokens_ref.shape[1]
     peers, _, n_runs, width = parts[0].shape
     per_peer = count // peers
+    rows = share_ref.shape[1] - PAD
 
     @pl.when(run == 0)
     def _():
-        gate_ref[...] = jnp.zeros_like(gate_ref)
-        taps_grad_ref[...] = jnp.zeros_like(taps_grad_ref)
+        share_ref[...] = jnp.zeros_like(share_ref)
         for part, start in zip(parts, starts):
-            rows = part.shape[1] * n_runs
+            got = part.shape[1] * n_runs
             for peer in range(peers):
                 at = (peer * per_peer + start) * n_runs
                 for lane in range(held.shape[0]):
                     value = part[peer, :, :, lane * LANES : (lane + 1) * LANES]
-                    held[lane, pl.ds(at, rows), :] = value.reshape(rows, LANES).astype(F32)
+                    held[lane, pl.ds(at, got), :] = value.reshape(got, LANES).astype(F32)
 
     raw, tokens, low, high, conv, sig = conv_and_sig(tokens_ref, ends_ref, taps_ref, weight_ref)
     back_first = jnp.concatenate(
@@ -212,13 +228,14 @@
     )
     back_conv = contract_first(row_ref[0], back_first) * sig
     for j, value in enumerate((low, tokens, high)):
-        taps_grad_ref[j : j + 1] += jnp.sum(back_conv * value, axis=0, keepdims=True)
+        share_ref[j, rows : rows + 1] += jnp.sum(back_conv * value, axis=0, keepdims=True)
     back_gate = (back_conv * conv * (1.0 - sig)).astype(BF16)
-    gate_ref[...] += contract_first(raw, back_gate)
+    share_ref[:, :rows] += contract_first(raw, back_gate).reshape(QUARTERS, rows, width)
 
 
 def gradient_share(tokens, ends, taps, weight, row, parts):
     runs, length, width = tokens.shape
+    shape = (QUARTERS, weight.shape[0] // QUARTERS + PAD, width)
     counts = [part.shape[1] for part in parts]
     starts = [sum(counts[:i]) for i in range(len(counts))]
     return pl.pallas_call(
@@ -232,14 +249,8 @@
             pl.BlockSpec((1, length, length), lambda r: (r, 0, 0)),
         ]
         + [pl.BlockSpec(part.shape, lambda r: (0, 0, 0, 0)) for part in parts],
-        out_specs=[
-            pl.BlockSpec(weight.shape, lambda r: (0, 0)),
-            pl.BlockSpec((8, width), lambda r: (0, 0)),
-        ],
-        out_shape=[
-            jax.ShapeDtypeStruct(weight.shape, F32),
-            jax.ShapeDtypeStruct((8, width), F32),
-        ],
+        out_specs=pl.BlockSpec(shape, lambda r: (0, 0, 0)),
+        out_shape=jax.ShapeDtypeStruct(shape, F32),
         scratch_shapes=[pltpu.VMEM((width // LANES, length * runs, LANES), F32)],
         compiler_params=params(),
         cost_estimate=cost(
@@ -253,12 +264,34 @@
     return lax.all_to_all(block, "ctx", split_axis=0, concat_axis=0, tiled=True)
 
 
-def total(value, peers):
-    step = 1
+def swapped(value, step, peers):
+    return lax.ppermute(value, "ctx", [(i, i ^ step) for i in range(peers)])
+
+
+def summed_quarter(share, peers):
+    own = lax.axis_index("ctx") % QUARTERS
+    quarter = lax.dynamic_index_in_dim(share, own, 0, keepdims=False)
+    for step in range(1, QUARTERS):
+        other = lax.dynamic_index_in_dim(share, own ^ step, 0, keepdims=False)
+        quarter = quarter + swapped(other, step, peers)
+    step = QUARTERS
     while step < peers:
-        value = value + lax.ppermute(value, "ctx", [(i, i ^ step) for i in range(peers)])
+        quarter = quarter + swapped(quarter, step, peers)
         step *= 2
-    return value
+    return quarter
+
+
+def gathered(quarter, peers):
+    own = lax.axis_index("ctx") % QUARTERS
+    held = [quarter] + [swapped(quarter, step, peers) for step in range(1, QUARTERS)]
+    for bit in (1, 2):
+        odd = (own & bit) != 0
+        held = [jnp.where(odd, held[i ^ bit], held[i]) for i in range(QUARTERS)]
+    return held
+
+
+def split(count, parts):
+    return [count * part // sum(parts) for part in parts]
 
 
 def local(tokens, conv_taps, gate_weight, row_factor, col_factor, cotangent):
@@ -267,29 +300,40 @@
     runs, length, _ = row_factor.shape
     offsets = col_factor.shape[0]
     rows = tokens.reshape(runs, length, width)
-    up = [(i, i + 1) for i in range(peers - 1)]
-    down = [(i + 1, i) for i in range(peers - 1)]
-    low = lax.ppermute(tokens[-1:], "ctx", up)
-    high = lax.ppermute(tokens[:1], "ctx", down)
-
-    block = back_first_all(peers, col_factor, cotangent)
-    block, low, high = lax.optimization_barrier((block, low, high))
-    back_got = exchange(block)
+
+    back_got = []
+    start = 0
+    for count in split(offsets, BACK_PARTS):
+        block = back_first_part(peers, col_factor, cotangent, start, count)
+        if back_got:
+            up = [(i, i + 1) for i in range(peers - 1)]
+            down = [(i + 1, i) for i in range(peers - 1)]
+            low = lax.ppermute(tokens[-1:], "ctx", up)
+            high = lax.ppermute(tokens[:1], "ctx", down)
+            block, low, high, back_got[0] = lax.optimization_barrier((block, low, high, back_got[0]))
+        back_got.append(exchange(block))
+        start += count
 
     before = jnp.concatenate([low, rows[:-1, -1]], axis=0)
     after = jnp.concatenate([rows[1:, 0], high], axis=0)
     ends = jnp.stack([before, after], axis=1).astype(F32)
-    (sent,) = first_parts(peers, rows, ends, conv_taps, gate_weight, row_factor, (offsets,))
-    sent, back_got = lax.optimization_barrier((sent, back_got))
-    got = exchange(sent)
-
-    gate_share, taps_share = gradient_share(
-        rows, ends, conv_taps, gate_weight, row_factor, [back_got]
-    )
-    both = total(jnp.concatenate([gate_share, taps_share], axis=0), peers)
-    n_gate = gate_weight.shape[0]
-    gate_grad, conv_grad = both[:n_gate], both[n_gate : n_gate + conv_taps.shape[0]]
-    return (mixed_all(col_factor, got), conv_grad, gate_grad)
+    counts = split(offsets, FORWARD_PARTS)
+    sent = list(first_parts(peers, rows, ends, conv_taps, gate_weight, row_factor, counts))
+    sent[0], back_got[-1] = lax.optimization_barrier((sent[0], back_got[-1]))
+    got = [exchange(sent[0])]
+
+    share = gradient_share(rows, ends, conv_taps, gate_weight, row_factor, back_got)
+    quarter = summed_quarter(share, peers)
+    sent[1], got[0], quarter = lax.optimization_barrier((sent[1], got[0], quarter))
+    got.append(exchange(sent[1]))
+    held = gathered(quarter, peers)
+    n_rows = quarter.shape[0] - PAD
+    gate_grad = jnp.concatenate([part[:n_rows] for part in held], axis=0)
+    conv_grad = jnp.concatenate([part[n_rows : n_rows + 1] for part in held[: conv_taps.shape[0]]], axis=0)
+
+    mixed = mixed_part(col_factor, got[0], 0, None)
+    mixed = mixed_part(col_factor, got[1], counts[0], mixed)
+    return (mixed, conv_grad, gate_grad)
 
 
 def solution(mesh):

time: 232 us -> 223 us (0.961)
  waiting for transfers between devices: 129 us -> 107 us
  starting transfers between devices: 45.4 us -> 50.9 us
  Pallas kernels: 51 us -> 54.4 us
    ppermute x4 -> x8, waiting for transfers between devices: 70.4 us -> 44.5 us  [swapped(): return lax.ppermute(value, 'ctx', [(i, i ^ step) for i in range(peers)])]
    all_to_all x2 -> x4, starting transfers between devices: 27.7 us -> 33.1 us  [exchange(): return lax.all_to_all(block, 'ctx', split_axis=0, concat_axis=0, tiled=True)]
    all_to_all x2 -> x4, waiting for transfers between devices: 58.2 us -> 62.9 us  [exchange(): return lax.all_to_all(block, 'ctx', split_axis=0, concat_axis=0, tiled=True)]
    pallas_call x2 -> x4, Pallas kernels: 11.3 us -> 14.5 us  [the longest x2 7.27 us: back_first_part(): pl.pallas_call(functools.partial(back_first_kernel, peers, GROUP, start),...]
    ppermute x4 -> x8, starting transfers between devices: 11 us -> 12 us  [swapped(): return lax.ppermute(value, 'ctx', [(i, i ^ step) for i in range(peers)])]
  transfers between devices with their start and end apart: 8 -> 14, of which waited for: 5 -> 8; matrix products, arithmetic and copies ran while one was open for 2% -> 3% of each run, Pallas kernels for 20% -> 22%
where the time goes in v3:
time: 223 us; the launch traced here: 221 us
  waiting for transfers between devices  107 us (48%)
  Pallas kernels  54.4 us (24%)
  starting transfers between devices  50.9 us (23%)
  local copies, waits for them, and re-layouts  4.74 us (2%)
  other arithmetic  2.96 us (1%)
    all_to_all x4, waiting for transfers between devices, exchange(): return lax.all_to_all(block, 'ctx', split_axis=0, concat_axis=0, tiled=True)  62.9 us
    ppermute x8, waiting for transfers between devices, swapped(): return lax.ppermute(value, 'ctx', [(i, i ^ step) for i in range(peers)])  44.5 us
    all_to_all x4, starting transfers between devices, exchange(): return lax.all_to_all(block, 'ctx', split_axis=0, concat_axis=0, tiled=True)  33.1 us
    pallas_call x1, Pallas kernels, gradient_share(): pl.pallas_call(functools.partial(gradient_kernel, starts), grid=(runs,),...  20.9 us
    pallas_call x1, Pallas kernels, first_parts(): pl.pallas_call(functools.partial(first_kernel, peers, starts), grid=(runs...  19 us
    ppermute x8, starting transfers between devices, swapped(): return lax.ppermute(value, 'ctx', [(i, i ^ step) for i in range(peers)])  12 us
    pallas_call x2, Pallas kernels, back_first_part(): pl.pallas_call(functools.partial(back_first_kernel, peers, GROUP, start),...  7.27 us
    pallas_call x2, Pallas kernels, mixed_part(): pl.pallas_call(functools.partial(mixed_kernel, GROUP, start), in_specs=[p...  7.25 us
  transfers between devices with their start and end apart: 14, of which 8 were waited for; matrix products, arithmetic and copies ran while one was open for 3% of the time, Pallas kernels for 22%

profile of v3, /device:TPU:0, one launch (start us, length us, event | category | flops | bytes accessed | tf_op | source)
XLA Modules:
  0.0 221.3 jit_solution(15292771460430369551)
XLA Ops:
  0.6 2.7 %shard_map.86 = bf16[16,8,16,256]{3,2,1,0:T(8,128)(2,1)} custom-call(bf16[32,256,256]{2,1,0:T(8,128)(2,1)} %col.7, bf16[32,256,256]{2,1,0:T(8,128)(2,1)} %cot.3), custom_call_target="tpu_custom_call" | custom-call | flops 268435456 | bytes 3145728 | tf_op jit(solution)/shard_map/pallas_call | solution.py:72
  3.4 8.3 %all-to-all-start = ((bf16[16,8,16,256]{3,2,1,0:T(8,128)(2,1)}), bf16[16,8,16,256]{3,2,1,0:T(8,128)(2,1)S(1)}, u32[]{:S(2)}, u32[]{:S(2)}) async-start(bf16[16,8,16,256]{3,2,1,0:T(8,128)(2,1)} %shard_map.86), calls=%async_computation | async-start | bytes 2097152 | tf_op jit(solution)/shard_map/all_to_all | solution.py:264
  11.7 0.7 fusion.3
  12.4 1.3 collective-permute-start.1
  13.7 4.5 %collective-permute-start = (bf16[1,256]{1,0:T(2,128)(2,1)S(1)}, bf16[1,256]{1,0:T(2,128)(2,1)S(1)}, u32[]{:S(2)}, u32[]{:S(2)}) collective-permute-start(bf16[1,256]{1,0:T(2,128)(2,1)S(1)} %get-tuple-element.31), channel_id=1, source_target_pairs={{0,2},{2,4},{4,6},{6,8},{8,10},{10,12},{12,14},{14,16},{16,18},{18... | collective-permute-start | bytes 1544 | tf_op jit(solution)/shard_map/ppermute | solution.py:311
  18.3 4.5 %shard_map.85 = bf16[16,24,16,256]{3,2,1,0:T(8,128)(2,1)} custom-call(bf16[32,256,256]{2,1,0:T(8,128)(2,1)} %col.7, bf16[32,256,256]{2,1,0:T(8,128)(2,1)} %cot.3), custom_call_target="tpu_custom_call" | custom-call | flops 805306368 | bytes 9437184 | tf_op jit(solution)/shard_map/pallas_call | solution.py:72
  22.8 13.3 %all-to-all-done.refs_0_ = bf16[16,8,16,256]{3,2,1,0:T(8,128)(2,1)S(1)} async-done(((bf16[16,8,16,256]{3,2,1,0:T(8,128)(2,1)}), bf16[16,8,16,256]{3,2,1,0:T(8,128)(2,1)S(1)}, u32[]{:S(2)}, u32[]{:S(2)}) %all-to-all-start) | async-done | bytes 1048608 | tf_op jit(solution)/shard_map/all_to_all | solution.py:264
  36.2 1.1 copy-done.1
  37.2 5.8 %all-to-all-start.1 = ((bf16[16,24,16,256]{3,2,1,0:T(8,128)(2,1)}), bf16[16,24,16,256]{3,2,1,0:T(8,128)(2,1)S(1)}, u32[]{:S(2)}, u32[]{:S(2)}) async-start(bf16[16,24,16,256]{3,2,1,0:T(8,128)(2,1)} %shard_map.85), calls=%async_computation.1 | async-start | bytes 6291456 | tf_op jit(solution)/shard_map/all_to_all | solution.py:264
  43.1 0.9 fusion.2
  44.7 19.0 %shard_map.87 = (bf16[16,24,16,256]{3,2,1,0:T(8,128)(2,1)}, bf16[16,8,16,256]{3,2,1,0:T(8,128)(2,1)}) custom-call(bf16[16,512,256]{2,1,0:T(8,128)(2,1)} %bitcast.24, f32[16,2,256]{2,1,0:T(2,128)} %maximum_convert_fusion.ends_ref, f32[3,256]{1,0:T(4,128)} %taps_ref.3, bf16[256,256]{1,0:T(8,128)(2,1)} %weight_ref.3, bf16[16,512,512]{2,1,0:T(8,128)(2,1)} %row_ref.3), custom_call_target="tpu_custom_call" | custom-call | flops 3221225472 | bytes 16777216 | tf_op jit(solution)/shard_map/pallas_call | solution.py:186
  63.7 39.4 %all-to-all-done.1.refs_1_ = bf16[16,24,16,256]{3,2,1,0:T(8,128)(2,1)S(1)} async-done(((bf16[16,24,16,256]{3,2,1,0:T(8,128)(2,1)}), bf16[16,24,16,256]{3,2,1,0:T(8,128)(2,1)S(1)}, u32[]{:S(2)}, u32[]{:S(2)}) %all-to-all-start.1) | async-done | bytes 3145760 | tf_op jit(solution)/shard_map/all_to_all | solution.py:264
  103.1 14.0 %all-to-all-start.2 = ((bf16[16,24,16,256]{3,2,1,0:T(8,128)(2,1)}), bf16[16,24,16,256]{3,2,1,0:T(8,128)(2,1)}, u32[]{:S(2)}, u32[]{:S(2)}) async-start(bf16[16,24,16,256]{3,2,1,0:T(8,128)(2,1)} %get-tuple-element.19), calls=%async_computation.2 | async-start | bytes 6291456 | tf_op jit(solution)/shard_map/all_to_all | solution.py:264
  117.1 20.9 %shard_map.88 = f32[4,72,256]{2,1,0:T(8,128)} custom-call(bf16[16,512,256]{2,1,0:T(8,128)(2,1)} %bitcast.25, f32[16,2,256]{2,1,0:T(2,128)} %maximum_convert_fusion.ends_ref, f32[3,256]{1,0:T(4,128)} %taps_ref.3, bf16[256,256]{1,0:T(8,128)(2,1)} %weight_ref.3, bf16[16,512,512]{2,1,0:T(8,128)(2,1)} %row_ref.3, bf16[16,8,16,256]{3,2,1,0:T(8,128)(2,1)} %copy-done.1, ...), custom_call_target="tpu_custom_call" | custom-call | flops 4294967296 | bytes 16777216 | tf_op jit(solution)/shard_map/pallas_call | solution.py:241
  138.0 1.0 dynamic-slice_bitcast_fusion.2
  139.0 1.9 collective-permute-start.2
  140.9 1.5 collective-permute-start.4
  142.6 1.6 collective-permute-done.2
  144.2 16.1 %collective-permute-done.4 = f32[72,256]{1,0:T(8,128)S(1)} collective-permute-done((f32[72,256]{1,0:T(8,128)S(1)}, f32[72,256]{1,0:T(8,128)S(1)}, u32[]{:S(2)}, u32[]{:S(2)}) %collective-permute-start.4) | collective-permute-done | bytes 73760 | tf_op jit(solution)/shard_map/ppermute | solution.py:268
  160.3 0.9 fusion.1
  161.3 7.4 %collective-permute-done.5 = f32[72,256]{1,0:T(8,128)S(1)} collective-permute-done((f32[72,256]{1,0:T(8,128)S(1)}, f32[72,256]{1,0:T(8,128)S(1)}, u32[]{:S(2)}, u32[]{:S(2)}) %collective-permute-start.5) | collective-permute-done | bytes 73760 | tf_op jit(solution)/shard_map/ppermute | solution.py:268
  168.7 4.8 %collective-permute-start.6 = (f32[72,256]{1,0:T(8,128)S(1)}, f32[72,256]{1,0:T(8,128)S(1)}, u32[]{:S(2)}, u32[]{:S(2)}) collective-permute-start(f32[72,256]{1,0:T(8,128)S(1)} %add.41), channel_id=1, source_target_pairs={{0,16},{2,18},{4,20},{6,22},{8,24},{10,26},{12,28},{14,30},{16,0},... | collective-permute-start | bytes 221192 | tf_op jit(solution)/shard_map/ppermute | solution.py:268
  173.5 16.6 %collective-permute-done.6 = f32[72,256]{1,0:T(8,128)S(1)} collective-permute-done((f32[72,256]{1,0:T(8,128)S(1)}, f32[72,256]{1,0:T(8,128)S(1)}, u32[]{:S(2)}, u32[]{:S(2)}) %collective-permute-start.6) | collective-permute-done | bytes 73760 | tf_op jit(solution)/shard_map/ppermute | solution.py:268
  190.1 4.9 %all-to-all-start.3 = ((bf16[16,8,16,256]{3,2,1,0:T(8,128)(2,1)}), bf16[16,8,16,256]{3,2,1,0:T(8,128)(2,1)S(1)}, u32[]{:S(2)}, u32[]{:S(2)}) async-start(bf16[16,8,16,256]{3,2,1,0:T(8,128)(2,1)} %get-tuple-element.22), calls=%async_computation.3 | async-start | bytes 2097152 | tf_op jit(solution)/shard_map/all_to_all | solution.py:264
  195.1 1.9 collective-permute-start.9
  197.0 1.5 collective-permute-start.8
  198.6 4.6 %shard_map.89.refs_0_ = bf16[32,256,256]{2,1,0:T(8,128)(2,1)} custom-call(bf16[32,256,256]{2,1,0:T(8,128)(2,1)} %col.7, bf16[16,24,16,256]{3,2,1,0:T(8,128)(2,1)} %all-to-all-done.2.recv), custom_call_target="tpu_custom_call" | custom-call | flops 805306368 | bytes 9437184 | tf_op jit(solution)/shard_map/pallas_call | solution.py:122
  203.2 2.8 %collective-permute-done.8 = f32[72,256]{1,0:T(8,128)S(1)} collective-permute-done((f32[72,256]{1,0:T(8,128)S(1)}, f32[72,256]{1,0:T(8,128)S(1)}, u32[]{:S(2)}, u32[]{:S(2)}) %collective-permute-start.8) | collective-permute-done | bytes 73760 | tf_op jit(solution)/shard_map/ppermute | solution.py:268
  206.7 0.7 pad_maximum_fusion
  207.5 10.2 %all-to-all-done.3.recv = bf16[16,8,16,256]{3,2,1,0:T(8,128)(2,1)S(1)} async-done(((bf16[16,8,16,256]{3,2,1,0:T(8,128)(2,1)}), bf16[16,8,16,256]{3,2,1,0:T(8,128)(2,1)S(1)}, u32[]{:S(2)}, u32[]{:S(2)}) %all-to-all-start.3) | async-done | bytes 1048608 | tf_op jit(solution)/shard_map/all_to_all | solution.py:264
  217.6 1.0 copy-done.2
  218.7 2.7 %shard_map.90 = bf16[32,256,256]{2,1,0:T(8,128)(2,1)} custom-call(bf16[32,256,256]{2,1,0:T(8,128)(2,1)} %col.7, bf16[16,8,16,256]{3,2,1,0:T(8,128)(2,1)} %copy-done.2, bf16[32,256,256]{2,1,0:T(8,128)(2,1)} %shard_map.89.refs_0_), custom_call_target="tpu_custom_call", output_to_operand_aliasing={{}: (2, {})} | custom-call | flops 268435456 | bytes 3145728 | tf_op jit(solution)/shard_map/pallas_call | solution.py:122
  (30 shorter events, 1.8 us)
Async XLA Ops:
  3.4 32.8 %all-to-all-start = ((bf16[16,8,16,256]{3,2,1,0:T(8,128)(2,1)}), bf16[16,8,16,256]{3,2,1,0:T(8,128)(2,1)S(1)}, u32[]{:S(2)}, u32[]{:S(2)}) async-start(bf16[16,8,16,256]{3,2,1,0:T(8,128)(2,1)} %shard_map.86), calls=%async_computation | async-start | bytes 2097152 | tf_op jit(solution)/shard_map/all_to_all | solution.py:264
  12.4 10.4 %collective-permute-start.1 = (bf16[1,256]{1,0:T(2,128)(2,1)S(1)}, bf16[1,256]{1,0:T(2,128)(2,1)S(1)}, u32[]{:S(2)}, u32[]{:S(2)}) collective-permute-start(bf16[1,256]{1,0:T(2,128)(2,1)S(1)} %get-tuple-element.30), channel_id=1, source_target_pairs={{2,0},{4,2},{6,4},{8,6},{10,8},{12,10},{14,12},{16,14},{18,16},{20... | collective-permute-start | bytes 1544 | tf_op jit(solution)/shard_map/ppermute | solution.py:312
  13.7 9.1 %collective-permute-start = (bf16[1,256]{1,0:T(2,128)(2,1)S(1)}, bf16[1,256]{1,0:T(2,128)(2,1)S(1)}, u32[]{:S(2)}, u32[]{:S(2)}) collective-permute-start(bf16[1,256]{1,0:T(2,128)(2,1)S(1)} %get-tuple-element.31), channel_id=1, source_target_pairs={{0,2},{2,4},{4,6},{6,8},{8,10},{10,12},{12,14},{14,16},{16,18},{18... | collective-permute-start | bytes 1544 | tf_op jit(solution)/shard_map/ppermute | solution.py:311
  36.2 1.1 copy-start.1
  37.2 65.8 %all-to-all-start.1 = ((bf16[16,24,16,256]{3,2,1,0:T(8,128)(2,1)}), bf16[16,24,16,256]{3,2,1,0:T(8,128)(2,1)S(1)}, u32[]{:S(2)}, u32[]{:S(2)}) async-start(bf16[16,24,16,256]{3,2,1,0:T(8,128)(2,1)} %shard_map.85), calls=%async_computation.1 | async-start | bytes 6291456 | tf_op jit(solution)/shard_map/all_to_all | solution.py:264
  103.1 14.1 %copy-start = (bf16[16,24,16,256]{3,2,1,0:T(8,128)(2,1)}, bf16[16,24,16,256]{3,2,1,0:T(8,128)(2,1)S(1)}, u32[]{:S(2)}) copy-start(bf16[16,24,16,256]{3,2,1,0:T(8,128)(2,1)S(1)} %all-to-all-done.1.refs_1_) | copy-start | bytes 9437188
  103.1 87.0 %all-to-all-start.2 = ((bf16[16,24,16,256]{3,2,1,0:T(8,128)(2,1)}), bf16[16,24,16,256]{3,2,1,0:T(8,128)(2,1)}, u32[]{:S(2)}, u32[]{:S(2)}) async-start(bf16[16,24,16,256]{3,2,1,0:T(8,128)(2,1)} %get-tuple-element.19), calls=%async_computation.2 | async-start | bytes 6291456 | tf_op jit(solution)/shard_map/all_to_all | solution.py:264
  139.0 5.2 %collective-permute-start.2 = (f32[72,256]{1,0:T(8,128)S(1)}, f32[72,256]{1,0:T(8,128)S(1)}, u32[]{:S(2)}, u32[]{:S(2)}) collective-permute-start(f32[72,256]{1,0:T(8,128)S(1)} %get-tuple-element.34), channel_id=1, source_target_pairs={{0,2},{2,0},{4,6},{6,4},{8,10},{10,8},{12,14},{14,12},{16,18},{18,... | collective-permute-start | bytes 221192 | tf_op jit(solution)/shard_map/ppermute | solution.py:268
  140.9 19.4 %collective-permute-start.4 = (f32[72,256]{1,0:T(8,128)S(1)}, f32[72,256]{1,0:T(8,128)S(1)}, u32[]{:S(2)}, u32[]{:S(2)}) collective-permute-start(f32[72,256]{1,0:T(8,128)S(1)} %get-tuple-element.35), channel_id=1, source_target_pairs={{0,6},{2,4},{4,2},{6,0},{8,14},{10,12},{12,10},{14,8},{16,22},{18,... | collective-permute-start | bytes 221192 | tf_op jit(solution)/shard_map/ppermute | solution.py:268
  142.4 17.9 %collective-permute-start.3 = (f32[72,256]{1,0:T(8,128)S(1)}, f32[72,256]{1,0:T(8,128)S(1)}, u32[]{:S(2)}, u32[]{:S(2)}) collective-permute-start(f32[72,256]{1,0:T(8,128)S(1)} %get-tuple-element.36), channel_id=1, source_target_pairs={{0,4},{2,6},{4,0},{6,2},{8,12},{10,14},{12,8},{14,10},{16,20},{18,... | collective-permute-start | bytes 221192 | tf_op jit(solution)/shard_map/ppermute | solution.py:268
  161.2 7.4 %collective-permute-start.5 = (f32[72,256]{1,0:T(8,128)S(1)}, f32[72,256]{1,0:T(8,128)S(1)}, u32[]{:S(2)}, u32[]{:S(2)}) collective-permute-start(f32[72,256]{1,0:T(8,128)S(1)} %fusion.1), channel_id=1, source_target_pairs={{0,8},{2,10},{4,12},{6,14},{8,0},{10,2},{12,4},{14,6},{16,24},{18,... | collective-permute-start | bytes 221192 | tf_op jit(solution)/shard_map/ppermute | solution.py:268
  168.7 21.4 %collective-permute-start.6 = (f32[72,256]{1,0:T(8,128)S(1)}, f32[72,256]{1,0:T(8,128)S(1)}, u32[]{:S(2)}, u32[]{:S(2)}) collective-permute-start(f32[72,256]{1,0:T(8,128)S(1)} %add.41), channel_id=1, source_target_pairs={{0,16},{2,18},{4,20},{6,22},{8,24},{10,26},{12,28},{14,30},{16,0},... | collective-permute-start | bytes 221192 | tf_op jit(solution)/shard_map/ppermute | solution.py:268
  190.1 27.5 %all-to-all-start.3 = ((bf16[16,8,16,256]{3,2,1,0:T(8,128)(2,1)}), bf16[16,8,16,256]{3,2,1,0:T(8,128)(2,1)S(1)}, u32[]{:S(2)}, u32[]{:S(2)}) async-start(bf16[16,8,16,256]{3,2,1,0:T(8,128)(2,1)} %get-tuple-element.22), calls=%async_computation.3 | async-start | bytes 2097152 | tf_op jit(solution)/shard_map/all_to_all | solution.py:264
  195.1 8.2 %collective-permute-start.9 = (f32[72,256]{1,0:T(8,128)S(1)}, f32[72,256]{1,0:T(8,128)S(1)}, u32[]{:S(2)}, u32[]{:S(2)}) collective-permute-start(f32[72,256]{1,0:T(8,128)S(1)} %add.42), channel_id=1, source_target_pairs={{0,2},{2,0},{4,6},{6,4},{8,10},{10,8},{12,14},{14,12},{16,18},{18,... | collective-permute-start | bytes 221192 | tf_op jit(solution)/shard_map/ppermute | solution.py:268
  197.0 9.0 %collective-permute-start.8 = (f32[72,256]{1,0:T(8,128)S(1)}, f32[72,256]{1,0:T(8,128)S(1)}, u32[]{:S(2)}, u32[]{:S(2)}) collective-permute-start(f32[72,256]{1,0:T(8,128)S(1)} %add.42), channel_id=1, source_target_pairs={{0,4},{2,6},{4,0},{6,2},{8,12},{10,14},{12,8},{14,10},{16,20},{18,... | collective-permute-start | bytes 221192 | tf_op jit(solution)/shard_map/ppermute | solution.py:268
  198.4 7.6 %collective-permute-start.7 = (f32[72,256]{1,0:T(8,128)S(1)}, f32[72,256]{1,0:T(8,128)S(1)}, u32[]{:S(2)}, u32[]{:S(2)}) collective-permute-start(f32[72,256]{1,0:T(8,128)S(1)} %add.42), channel_id=1, source_target_pairs={{0,6},{2,4},{4,2},{6,0},{8,14},{10,12},{12,10},{14,8},{16,22},{18,... | collective-permute-start | bytes 221192 | tf_op jit(solution)/shard_map/ppermute | solution.py:268
  217.6 1.0 copy-start.2

commit v4 on v3

--- a/solution.py
+++ b/solution.py
@@ -15,7 +15,7 @@
 PAD = 8
 BACK_PARTS = (1, 3)
 FORWARD_PARTS = (3, 1)
-VMEM_LIMIT = 60 * 1024 * 1024
+VMEM_LIMIT = 63 * 1024 * 1024 + 768 * 1024
 
 
 def params():

time: 223 us -> 221 us (level)
  no operation moved by 1% of the time
where the time goes in v4:
time: 221 us; the launch traced here: 219 us
  waiting for transfers between devices  107 us (48%)
  Pallas kernels  54.3 us (25%)
  starting transfers between devices  51.2 us (23%)
  other arithmetic  3.89 us (2%)
  local copies, waits for them, and re-layouts  2.64 us (1%)
    all_to_all x4, waiting for transfers between devices, exchange(): return lax.all_to_all(block, 'ctx', split_axis=0, concat_axis=0, tiled=True)  61.8 us
    ppermute x8, waiting for transfers between devices, swapped(): return lax.ppermute(value, 'ctx', [(i, i ^ step) for i in range(peers)])  44.8 us
    all_to_all x4, starting transfers between devices, exchange(): return lax.all_to_all(block, 'ctx', split_axis=0, concat_axis=0, tiled=True)  33.2 us
    pallas_call x1, Pallas kernels, gradient_share(): pl.pallas_call(functools.partial(gradient_kernel, starts), grid=(runs,),...  20.9 us
    pallas_call x1, Pallas kernels, first_parts(): pl.pallas_call(functools.partial(first_kernel, peers, starts), grid=(runs...  19 us
    ppermute x8, starting transfers between devices, swapped(): return lax.ppermute(value, 'ctx', [(i, i ^ step) for i in range(peers)])  12.1 us
    pallas_call x2, Pallas kernels, mixed_part(): pl.pallas_call(functools.partial(mixed_kernel, GROUP, start), in_specs=[p...  7.25 us
    pallas_call x2, Pallas kernels, back_first_part(): pl.pallas_call(functools.partial(back_first_kernel, peers, GROUP, start),...  7.2 us
  transfers between devices with their start and end apart: 14, of which 8 were waited for; matrix products, arithmetic and copies ran while one was open for 3% of the time, Pallas kernels for 22%

profile of v4, /device:TPU:0, one launch (start us, length us, event | category | flops | bytes accessed | tf_op | source)
XLA Modules:
  0.0 219.5 jit_solution(8697062920093325018)
XLA Ops:
  0.6 2.7 %shard_map.86 = bf16[16,8,16,256]{3,2,1,0:T(8,128)(2,1)} custom-call(bf16[32,256,256]{2,1,0:T(8,128)(2,1)} %col.7, bf16[32,256,256]{2,1,0:T(8,128)(2,1)} %cot.3), custom_call_target="tpu_custom_call" | custom-call | flops 268435456 | bytes 3145728 | tf_op jit(solution)/shard_map/pallas_call | solution.py:72
  3.4 8.4 %all-to-all-start = ((bf16[16,8,16,256]{3,2,1,0:T(8,128)(2,1)}), bf16[16,8,16,256]{3,2,1,0:T(8,128)(2,1)}, u32[]{:S(2)}, u32[]{:S(2)}) async-start(bf16[16,8,16,256]{3,2,1,0:T(8,128)(2,1)} %shard_map.86), calls=%async_computation | async-start | bytes 2097152 | tf_op jit(solution)/shard_map/all_to_all | solution.py:264
  11.8 0.7 fusion.3
  12.5 1.3 collective-permute-start.1
  13.8 4.5 %collective-permute-start = (bf16[1,256]{1,0:T(2,128)(2,1)S(1)}, bf16[1,256]{1,0:T(2,128)(2,1)S(1)}, u32[]{:S(2)}, u32[]{:S(2)}) collective-permute-start(bf16[1,256]{1,0:T(2,128)(2,1)S(1)} %get-tuple-element.31), channel_id=1, source_target_pairs={{0,2},{2,4},{4,6},{6,8},{8,10},{10,12},{12,14},{14,16},{16,18},{18... | collective-permute-start | bytes 1544 | tf_op jit(solution)/shard_map/ppermute | solution.py:311
  18.3 4.5 %shard_map.85 = bf16[16,24,16,256]{3,2,1,0:T(8,128)(2,1)} custom-call(bf16[32,256,256]{2,1,0:T(8,128)(2,1)} %col.7, bf16[32,256,256]{2,1,0:T(8,128)(2,1)} %cot.3), custom_call_target="tpu_custom_call" | custom-call | flops 805306368 | bytes 9437184 | tf_op jit(solution)/shard_map/pallas_call | solution.py:72
  22.8 13.5 %all-to-all-done.refs_0_ = bf16[16,8,16,256]{3,2,1,0:T(8,128)(2,1)} async-done(((bf16[16,8,16,256]{3,2,1,0:T(8,128)(2,1)}), bf16[16,8,16,256]{3,2,1,0:T(8,128)(2,1)}, u32[]{:S(2)}, u32[]{:S(2)}) %all-to-all-start) | async-done | bytes 1048608 | tf_op jit(solution)/shard_map/all_to_all | solution.py:264
  36.3 5.9 %all-to-all-start.1 = ((bf16[16,24,16,256]{3,2,1,0:T(8,128)(2,1)}), bf16[16,24,16,256]{3,2,1,0:T(8,128)(2,1)}, u32[]{:S(2)}, u32[]{:S(2)}) async-start(bf16[16,24,16,256]{3,2,1,0:T(8,128)(2,1)} %shard_map.85), calls=%async_computation.1 | async-start | bytes 6291456 | tf_op jit(solution)/shard_map/all_to_all | solution.py:264
  42.1 0.9 fusion.2
  43.1 0.7 maximum_convert_fusion.ends_ref
  43.8 19.0 %shard_map.87 = (bf16[16,24,16,256]{3,2,1,0:T(8,128)(2,1)}, bf16[16,8,16,256]{3,2,1,0:T(8,128)(2,1)}) custom-call(bf16[16,512,256]{2,1,0:T(8,128)(2,1)} %bitcast.24, f32[16,2,256]{2,1,0:T(2,128)} %maximum_convert_fusion.ends_ref, f32[3,256]{1,0:T(4,128)} %taps_ref.3, bf16[256,256]{1,0:T(8,128)(2,1)} %weight_ref.3, bf16[16,512,512]{2,1,0:T(8,128)(2,1)} %row_ref.3), custom_call_target="tpu_custom_call" | custom-call | flops 3221225472 | bytes 16777216 | tf_op jit(solution)/shard_map/pallas_call | solution.py:186
  62.8 39.3 %all-to-all-done.1.refs_1_ = bf16[16,24,16,256]{3,2,1,0:T(8,128)(2,1)} async-done(((bf16[16,24,16,256]{3,2,1,0:T(8,128)(2,1)}), bf16[16,24,16,256]{3,2,1,0:T(8,128)(2,1)}, u32[]{:S(2)}, u32[]{:S(2)}) %all-to-all-start.1) | async-done | bytes 3145760 | tf_op jit(solution)/shard_map/all_to_all | solution.py:264
  102.0 14.0 %all-to-all-start.2 = ((bf16[16,24,16,256]{3,2,1,0:T(8,128)(2,1)}), bf16[16,24,16,256]{3,2,1,0:T(8,128)(2,1)}, u32[]{:S(2)}, u32[]{:S(2)}) async-start(bf16[16,24,16,256]{3,2,1,0:T(8,128)(2,1)} %get-tuple-element.19), calls=%async_computation.2 | async-start | bytes 6291456 | tf_op jit(solution)/shard_map/all_to_all | solution.py:264
  116.1 20.9 %shard_map.88 = f32[4,72,256]{2,1,0:T(8,128)} custom-call(bf16[16,512,256]{2,1,0:T(8,128)(2,1)} %bitcast.25, f32[16,2,256]{2,1,0:T(2,128)} %maximum_convert_fusion.ends_ref, f32[3,256]{1,0:T(4,128)} %taps_ref.3, bf16[256,256]{1,0:T(8,128)(2,1)} %weight_ref.3, bf16[16,512,512]{2,1,0:T(8,128)(2,1)} %row_ref.3, bf16[16,8,16,256]{3,2,1,0:T(8,128)(2,1)} %all-to-all-done.refs_0_, ...), custom_call_target="tpu_custom_call" | custom-call | flops 4294967296 | bytes 16777216 | tf_op jit(solution)/shard_map/pallas_call | solution.py:241
  136.9 1.0 dynamic-slice_bitcast_fusion.2
  137.9 1.9 collective-permute-start.2
  139.8 1.5 collective-permute-start.4
  141.5 1.5 collective-permute-done.2
  143.0 16.1 %collective-permute-done.4 = f32[72,256]{1,0:T(8,128)S(1)} collective-permute-done((f32[72,256]{1,0:T(8,128)S(1)}, f32[72,256]{1,0:T(8,128)S(1)}, u32[]{:S(2)}, u32[]{:S(2)}) %collective-permute-start.4) | collective-permute-done | bytes 73760 | tf_op jit(solution)/shard_map/ppermute | solution.py:268
  159.0 0.9 fusion.1
  160.0 7.4 %collective-permute-done.5 = f32[72,256]{1,0:T(8,128)S(1)} collective-permute-done((f32[72,256]{1,0:T(8,128)S(1)}, f32[72,256]{1,0:T(8,128)S(1)}, u32[]{:S(2)}, u32[]{:S(2)}) %collective-permute-start.5) | collective-permute-done | bytes 73760 | tf_op jit(solution)/shard_map/ppermute | solution.py:268
  167.5 4.9 %collective-permute-start.6 = (f32[72,256]{1,0:T(8,128)S(1)}, f32[72,256]{1,0:T(8,128)S(1)}, u32[]{:S(2)}, u32[]{:S(2)}) collective-permute-start(f32[72,256]{1,0:T(8,128)S(1)} %add.41), channel_id=1, source_target_pairs={{0,16},{2,18},{4,20},{6,22},{8,24},{10,26},{12,28},{14,30},{16,0},... | collective-permute-start | bytes 221192 | tf_op jit(solution)/shard_map/ppermute | solution.py:268
  172.4 16.5 %collective-permute-done.6 = f32[72,256]{1,0:T(8,128)S(1)} collective-permute-done((f32[72,256]{1,0:T(8,128)S(1)}, f32[72,256]{1,0:T(8,128)S(1)}, u32[]{:S(2)}, u32[]{:S(2)}) %collective-permute-start.6) | collective-permute-done | bytes 73760 | tf_op jit(solution)/shard_map/ppermute | solution.py:268
  188.9 5.0 %all-to-all-start.3 = ((bf16[16,8,16,256]{3,2,1,0:T(8,128)(2,1)}), bf16[16,8,16,256]{3,2,1,0:T(8,128)(2,1)}, u32[]{:S(2)}, u32[]{:S(2)}) async-start(bf16[16,8,16,256]{3,2,1,0:T(8,128)(2,1)} %get-tuple-element.22), calls=%async_computation.3 | async-start | bytes 2097152 | tf_op jit(solution)/shard_map/all_to_all | solution.py:264
  193.9 1.9 collective-permute-start.9
  195.8 1.5 collective-permute-start.8
  197.5 4.6 %shard_map.89.refs_0_ = bf16[32,256,256]{2,1,0:T(8,128)(2,1)} custom-call(bf16[32,256,256]{2,1,0:T(8,128)(2,1)} %col.7, bf16[16,24,16,256]{3,2,1,0:T(8,128)(2,1)} %all-to-all-done.2.recv), custom_call_target="tpu_custom_call" | custom-call | flops 805306368 | bytes 9437184 | tf_op jit(solution)/shard_map/pallas_call | solution.py:122
  202.1 3.3 %collective-permute-done.8 = f32[72,256]{1,0:T(8,128)} collective-permute-done((f32[72,256]{1,0:T(8,128)S(1)}, f32[72,256]{1,0:T(8,128)}, u32[]{:S(2)}, u32[]{:S(2)}) %collective-permute-start.8) | collective-permute-done | bytes 73760 | tf_op jit(solution)/shard_map/ppermute | solution.py:268
  205.4 1.0 broadcast_select_fusion.5
  207.0 0.7 pad_maximum_fusion
  207.7 9.0 %all-to-all-done.3.recv = bf16[16,8,16,256]{3,2,1,0:T(8,128)(2,1)} async-done(((bf16[16,8,16,256]{3,2,1,0:T(8,128)(2,1)}), bf16[16,8,16,256]{3,2,1,0:T(8,128)(2,1)}, u32[]{:S(2)}, u32[]{:S(2)}) %all-to-all-start.3) | async-done | bytes 1048608 | tf_op jit(solution)/shard_map/all_to_all | solution.py:264
  216.8 2.7 %shard_map.90 = bf16[32,256,256]{2,1,0:T(8,128)(2,1)} custom-call(bf16[32,256,256]{2,1,0:T(8,128)(2,1)} %col.7, bf16[16,8,16,256]{3,2,1,0:T(8,128)(2,1)} %all-to-all-done.3.recv, bf16[32,256,256]{2,1,0:T(8,128)(2,1)} %shard_map.89.refs_0_), custom_call_target="tpu_custom_call", output_to_operand_aliasing={{}: (2, {})} | custom-call | flops 268435456 | bytes 3145728 | tf_op jit(solution)/shard_map/pallas_call | solution.py:122
  (24 shorter events, 1.2 us)
Async XLA Ops:
  3.4 32.9 %all-to-all-start = ((bf16[16,8,16,256]{3,2,1,0:T(8,128)(2,1)}), bf16[16,8,16,256]{3,2,1,0:T(8,128)(2,1)}, u32[]{:S(2)}, u32[]{:S(2)}) async-start(bf16[16,8,16,256]{3,2,1,0:T(8,128)(2,1)} %shard_map.86), calls=%async_computation | async-start | bytes 2097152 | tf_op jit(solution)/shard_map/all_to_all | solution.py:264
  12.5 10.3 %collective-permute-start.1 = (bf16[1,256]{1,0:T(2,128)(2,1)S(1)}, bf16[1,256]{1,0:T(2,128)(2,1)S(1)}, u32[]{:S(2)}, u32[]{:S(2)}) collective-permute-start(bf16[1,256]{1,0:T(2,128)(2,1)S(1)} %get-tuple-element.30), channel_id=1, source_target_pairs={{2,0},{4,2},{6,4},{8,6},{10,8},{12,10},{14,12},{16,14},{18,16},{20... | collective-permute-start | bytes 1544 | tf_op jit(solution)/shard_map/ppermute | solution.py:312
  13.8 9.0 %collective-permute-start = (bf16[1,256]{1,0:T(2,128)(2,1)S(1)}, bf16[1,256]{1,0:T(2,128)(2,1)S(1)}, u32[]{:S(2)}, u32[]{:S(2)}) collective-permute-start(bf16[1,256]{1,0:T(2,128)(2,1)S(1)} %get-tuple-element.31), channel_id=1, source_target_pairs={{0,2},{2,4},{4,6},{6,8},{8,10},{10,12},{12,14},{14,16},{16,18},{18... | collective-permute-start | bytes 1544 | tf_op jit(solution)/shard_map/ppermute | solution.py:311
  36.3 65.8 %all-to-all-start.1 = ((bf16[16,24,16,256]{3,2,1,0:T(8,128)(2,1)}), bf16[16,24,16,256]{3,2,1,0:T(8,128)(2,1)}, u32[]{:S(2)}, u32[]{:S(2)}) async-start(bf16[16,24,16,256]{3,2,1,0:T(8,128)(2,1)} %shard_map.85), calls=%async_computation.1 | async-start | bytes 6291456 | tf_op jit(solution)/shard_map/all_to_all | solution.py:264
  102.0 86.9 %all-to-all-start.2 = ((bf16[16,24,16,256]{3,2,1,0:T(8,128)(2,1)}), bf16[16,24,16,256]{3,2,1,0:T(8,128)(2,1)}, u32[]{:S(2)}, u32[]{:S(2)}) async-start(bf16[16,24,16,256]{3,2,1,0:T(8,128)(2,1)} %get-tuple-element.19), calls=%async_computation.2 | async-start | bytes 6291456 | tf_op jit(solution)/shard_map/all_to_all | solution.py:264
  137.9 5.1 %collective-permute-start.2 = (f32[72,256]{1,0:T(8,128)S(1)}, f32[72,256]{1,0:T(8,128)S(1)}, u32[]{:S(2)}, u32[]{:S(2)}) collective-permute-start(f32[72,256]{1,0:T(8,128)S(1)} %get-tuple-element.34), channel_id=1, source_target_pairs={{0,2},{2,0},{4,6},{6,4},{8,10},{10,8},{12,14},{14,12},{16,18},{18,... | collective-permute-start | bytes 221192 | tf_op jit(solution)/shard_map/ppermute | solution.py:268
  139.8 19.2 %collective-permute-start.4 = (f32[72,256]{1,0:T(8,128)S(1)}, f32[72,256]{1,0:T(8,128)S(1)}, u32[]{:S(2)}, u32[]{:S(2)}) collective-permute-start(f32[72,256]{1,0:T(8,128)S(1)} %get-tuple-element.35), channel_id=1, source_target_pairs={{0,6},{2,4},{4,2},{6,0},{8,14},{10,12},{12,10},{14,8},{16,22},{18,... | collective-permute-start | bytes 221192 | tf_op jit(solution)/shard_map/ppermute | solution.py:268
  141.3 17.8 %collective-permute-start.3 = (f32[72,256]{1,0:T(8,128)S(1)}, f32[72,256]{1,0:T(8,128)S(1)}, u32[]{:S(2)}, u32[]{:S(2)}) collective-permute-start(f32[72,256]{1,0:T(8,128)S(1)} %get-tuple-element.36), channel_id=1, source_target_pairs={{0,4},{2,6},{4,0},{6,2},{8,12},{10,14},{12,8},{14,10},{16,20},{18,... | collective-permute-start | bytes 221192 | tf_op jit(solution)/shard_map/ppermute | solution.py:268
  159.9 7.5 %collective-permute-start.5 = (f32[72,256]{1,0:T(8,128)S(1)}, f32[72,256]{1,0:T(8,128)S(1)}, u32[]{:S(2)}, u32[]{:S(2)}) collective-permute-start(f32[72,256]{1,0:T(8,128)S(1)} %fusion.1), channel_id=1, source_target_pairs={{0,8},{2,10},{4,12},{6,14},{8,0},{10,2},{12,4},{14,6},{16,24},{18,... | collective-permute-start | bytes 221192 | tf_op jit(solution)/shard_map/ppermute | solution.py:268
  167.5 21.4 %collective-permute-start.6 = (f32[72,256]{1,0:T(8,128)S(1)}, f32[72,256]{1,0:T(8,128)S(1)}, u32[]{:S(2)}, u32[]{:S(2)}) collective-permute-start(f32[72,256]{1,0:T(8,128)S(1)} %add.41), channel_id=1, source_target_pairs={{0,16},{2,18},{4,20},{6,22},{8,24},{10,26},{12,28},{14,30},{16,0},... | collective-permute-start | bytes 221192 | tf_op jit(solution)/shard_map/ppermute | solution.py:268
  188.9 27.9 %all-to-all-start.3 = ((bf16[16,8,16,256]{3,2,1,0:T(8,128)(2,1)}), bf16[16,8,16,256]{3,2,1,0:T(8,128)(2,1)}, u32[]{:S(2)}, u32[]{:S(2)}) async-start(bf16[16,8,16,256]{3,2,1,0:T(8,128)(2,1)} %get-tuple-element.22), calls=%async_computation.3 | async-start | bytes 2097152 | tf_op jit(solution)/shard_map/all_to_all | solution.py:264
  193.9 8.2 %collective-permute-start.9 = (f32[72,256]{1,0:T(8,128)S(1)}, f32[72,256]{1,0:T(8,128)S(1)}, u32[]{:S(2)}, u32[]{:S(2)}) collective-permute-start(f32[72,256]{1,0:T(8,128)S(1)} %add.42), channel_id=1, source_target_pairs={{0,2},{2,0},{4,6},{6,4},{8,10},{10,8},{12,14},{14,12},{16,18},{18,... | collective-permute-start | bytes 221192 | tf_op jit(solution)/shard_map/ppermute | solution.py:268
  195.8 9.6 %collective-permute-start.8 = (f32[72,256]{1,0:T(8,128)S(1)}, f32[72,256]{1,0:T(8,128)}, u32[]{:S(2)}, u32[]{:S(2)}) collective-permute-start(f32[72,256]{1,0:T(8,128)S(1)} %add.42), channel_id=1, source_target_pairs={{0,4},{2,6},{4,0},{6,2},{8,12},{10,14},{12,8},{14,10},{16,20},{18,... | collective-permute-start | bytes 221192 | tf_op jit(solution)/shard_map/ppermute | solution.py:268
  197.3 8.1 %collective-permute-start.7 = (f32[72,256]{1,0:T(8,128)S(1)}, f32[72,256]{1,0:T(8,128)}, u32[]{:S(2)}, u32[]{:S(2)}) collective-permute-start(f32[72,256]{1,0:T(8,128)S(1)} %add.42), channel_id=1, source_target_pairs={{0,6},{2,4},{4,2},{6,0},{8,14},{10,12},{12,10},{14,8},{16,22},{18,... | collective-permute-start | bytes 221192 | tf_op jit(solution)/shard_map/ppermute | solution.py:268

commit v5 on v4

--- a/solution.py
+++ b/solution.py
@@ -114,7 +114,7 @@
         store[0].wait()
 
 
-def mixed_part(col, recv, start, before):
+def mixed_part(col, recv, start, before, grant):
     offsets, order, runs_all = col.shape
     count, width = recv.shape[1], recv.shape[3]
     steps = count // GROUP
@@ -132,11 +132,44 @@
             pltpu.SemaphoreType.DMA((2 * steps,)),
             pltpu.SemaphoreType.DMA((steps,)),
         ],
-        compiler_params=params(),
+        compiler_params=pltpu.CompilerParams(vmem_limit_bytes=grant),
         cost_estimate=cost(
             2 * count * order * runs_all * width, 2 * count * (order * runs_all + 2 * order * width)
         ),
     )(*operands)
+
+
+def last_mixed_kernel(group, first, col, recv, before, out, out_held, sems):
+    peers, offsets, runs, width = recv.shape
+    stores = []
+    for start in range(0, offsets, group):
+        for d in range(start, start + group):
+            value = recv[:, d].reshape(peers * runs, width)
+            out_held[d] = jnp.dot(col[d], value, preferred_element_type=F32).astype(BF16)
+        pair = (out_held.at[pl.ds(start, group)], out.at[pl.ds(first + start, group)])
+        stores += copies([pair], sems, len(stores))
+        stores[-1].start()
+    for store in stores:
+        store.wait()
+
+
+def last_mixed_part(col, recv, start, before):
+    count, order, runs_all = col.shape
+    width = recv.shape[3]
+    steps = count // GROUP
+    vmem = pl.BlockSpec(memory_space=pltpu.VMEM)
+    return pl.pallas_call(
+        functools.partial(last_mixed_kernel, GROUP, start),
+        in_specs=[vmem, vmem, pl.BlockSpec(memory_space=pl.ANY)],
+        out_specs=pl.BlockSpec(memory_space=pl.ANY),
+        out_shape=jax.ShapeDtypeStruct(before.shape, BF16),
+        input_output_aliases={2: 0},
+        scratch_shapes=[pltpu.VMEM((count, order, width), BF16), pltpu.SemaphoreType.DMA((steps,))],
+        compiler_params=pltpu.CompilerParams(vmem_limit_bytes=VMEM_LIMIT // 4),
+        cost_estimate=cost(
+            2 * count * order * runs_all * width, 2 * count * (order * runs_all + 2 * order * width)
+        ),
+    )(col, recv, before)
 
 
 def shifted(tokens, before, after):
@@ -331,8 +364,9 @@
     gate_grad = jnp.concatenate([part[:n_rows] for part in held], axis=0)
     conv_grad = jnp.concatenate([part[n_rows : n_rows + 1] for part in held[: conv_taps.shape[0]]], axis=0)
 
-    mixed = mixed_part(col_factor, got[0], 0, None)
-    mixed = mixed_part(col_factor, got[1], counts[0], mixed)
+    mixed = mixed_part(col_factor, got[0], 0, None, VMEM_LIMIT // 4 * 3)
+    rest, _ = lax.optimization_barrier((col_factor[counts[0] :], quarter))
+    mixed = last_mixed_part(rest, got[1], counts[0], mixed)
     return (mixed, conv_grad, gate_grad)
 
 

time: 221 us -> 219 us (level)
    pallas_call x2 -> x1, Pallas kernels: 7.25 us -> 4.59 us  [mixed_part(): pl.pallas_call(functools.partial(mixed_kernel, GROUP, start), in_specs=[p...]
  transfers between devices with their start and end apart: 14 -> 14, of which waited for: 8 -> 9; matrix products, arithmetic and copies ran while one was open for 3% -> 3% of each run, Pallas kernels for 22% -> 22%
where the time goes in v5:
time: 219 us; the launch traced here: 218 us
  waiting for transfers between devices  106 us (48%)
  Pallas kernels  52.9 us (24%)
  starting transfers between devices  51.1 us (23%)
  local copies, waits for them, and re-layouts  3.94 us (2%)
  other arithmetic  2.96 us (1%)
    all_to_all x4, waiting for transfers between devices, exchange(): return lax.all_to_all(block, 'ctx', split_axis=0, concat_axis=0, tiled=True)  61.1 us
    ppermute x8, waiting for transfers between devices, swapped(): return lax.ppermute(value, 'ctx', [(i, i ^ step) for i in range(peers)])  44.8 us
    all_to_all x4, starting transfers between devices, exchange(): return lax.all_to_all(block, 'ctx', split_axis=0, concat_axis=0, tiled=True)  33.2 us
    pallas_call x1, Pallas kernels, gradient_share(): pl.pallas_call(functools.partial(gradient_kernel, starts), grid=(runs,),...  20.9 us
    pallas_call x1, Pallas kernels, first_parts(): pl.pallas_call(functools.partial(first_kernel, peers, starts), grid=(runs...  19 us
    ppermute x8, starting transfers between devices, swapped(): return lax.ppermute(value, 'ctx', [(i, i ^ step) for i in range(peers)])  12.1 us
    pallas_call x2, Pallas kernels, back_first_part(): pl.pallas_call(functools.partial(back_first_kernel, peers, GROUP, start),...  7.21 us
    pallas_call x1, Pallas kernels, mixed_part(): pl.pallas_call(functools.partial(mixed_kernel, GROUP, start), in_specs=[p...  4.59 us
  transfers between devices with their start and end apart: 14, of which 9 were waited for; matrix products, arithmetic and copies ran while one was open for 3% of the time, Pallas kernels for 22%

profile of v5, /device:TPU:0, one launch (start us, length us, event | category | flops | bytes accessed | tf_op | source)
XLA Modules:
  0.0 217.7 jit_solution(15256928282292511548)
XLA Ops:
  0.6 2.7 %shard_map.86 = bf16[16,8,16,256]{3,2,1,0:T(8,128)(2,1)} custom-call(bf16[32,256,256]{2,1,0:T(8,128)(2,1)} %col.5, bf16[32,256,256]{2,1,0:T(8,128)(2,1)} %cot.3), custom_call_target="tpu_custom_call" | custom-call | flops 268435456 | bytes 3145728 | tf_op jit(solution)/shard_map/pallas_call | solution.py:72
  3.4 8.4 %all-to-all-start = ((bf16[16,8,16,256]{3,2,1,0:T(8,128)(2,1)}), bf16[16,8,16,256]{3,2,1,0:T(8,128)(2,1)}, u32[]{:S(2)}, u32[]{:S(2)}) async-start(bf16[16,8,16,256]{3,2,1,0:T(8,128)(2,1)} %shard_map.86), calls=%async_computation | async-start | bytes 2097152 | tf_op jit(solution)/shard_map/all_to_all | solution.py:297
  11.8 0.7 fusion.3
  12.5 1.3 collective-permute-start.1
  13.8 4.5 %collective-permute-start = (bf16[1,256]{1,0:T(2,128)(2,1)S(1)}, bf16[1,256]{1,0:T(2,128)(2,1)S(1)}, u32[]{:S(2)}, u32[]{:S(2)}) collective-permute-start(bf16[1,256]{1,0:T(2,128)(2,1)S(1)} %get-tuple-element.33), channel_id=1, source_target_pairs={{0,2},{2,4},{4,6},{6,8},{8,10},{10,12},{12,14},{14,16},{16,18},{18... | collective-permute-start | bytes 1544 | tf_op jit(solution)/shard_map/ppermute | solution.py:344
  18.3 4.5 %shard_map.85 = bf16[16,24,16,256]{3,2,1,0:T(8,128)(2,1)} custom-call(bf16[32,256,256]{2,1,0:T(8,128)(2,1)} %col.5, bf16[32,256,256]{2,1,0:T(8,128)(2,1)} %cot.3), custom_call_target="tpu_custom_call" | custom-call | flops 805306368 | bytes 9437184 | tf_op jit(solution)/shard_map/pallas_call | solution.py:72
  22.8 13.4 %all-to-all-done.refs_0_ = bf16[16,8,16,256]{3,2,1,0:T(8,128)(2,1)} async-done(((bf16[16,8,16,256]{3,2,1,0:T(8,128)(2,1)}), bf16[16,8,16,256]{3,2,1,0:T(8,128)(2,1)}, u32[]{:S(2)}, u32[]{:S(2)}) %all-to-all-start) | async-done | bytes 1048608 | tf_op jit(solution)/shard_map/all_to_all | solution.py:297
  36.3 5.9 %all-to-all-start.1 = ((bf16[16,24,16,256]{3,2,1,0:T(8,128)(2,1)}), bf16[16,24,16,256]{3,2,1,0:T(8,128)(2,1)}, u32[]{:S(2)}, u32[]{:S(2)}) async-start(bf16[16,24,16,256]{3,2,1,0:T(8,128)(2,1)} %shard_map.85), calls=%async_computation.1 | async-start | bytes 6291456 | tf_op jit(solution)/shard_map/all_to_all | solution.py:297
  42.1 0.9 fusion.2
  43.1 0.7 maximum_convert_fusion.ends_ref
  43.8 19.0 %shard_map.87 = (bf16[16,24,16,256]{3,2,1,0:T(8,128)(2,1)}, bf16[16,8,16,256]{3,2,1,0:T(8,128)(2,1)}) custom-call(bf16[16,512,256]{2,1,0:T(8,128)(2,1)} %bitcast.24, f32[16,2,256]{2,1,0:T(2,128)} %maximum_convert_fusion.ends_ref, f32[3,256]{1,0:T(4,128)} %taps_ref.3, bf16[256,256]{1,0:T(8,128)(2,1)} %weight_ref.3, bf16[16,512,512]{2,1,0:T(8,128)(2,1)} %row_ref.3), custom_call_target="tpu_custom_call" | custom-call | flops 3221225472 | bytes 16777216 | tf_op jit(solution)/shard_map/pallas_call | solution.py:219
  62.8 39.3 %all-to-all-done.1.refs_1_ = bf16[16,24,16,256]{3,2,1,0:T(8,128)(2,1)} async-done(((bf16[16,24,16,256]{3,2,1,0:T(8,128)(2,1)}), bf16[16,24,16,256]{3,2,1,0:T(8,128)(2,1)}, u32[]{:S(2)}, u32[]{:S(2)}) %all-to-all-start.1) | async-done | bytes 3145760 | tf_op jit(solution)/shard_map/all_to_all | solution.py:297
  102.0 14.0 %all-to-all-start.2 = ((bf16[16,24,16,256]{3,2,1,0:T(8,128)(2,1)}), bf16[16,24,16,256]{3,2,1,0:T(8,128)(2,1)}, u32[]{:S(2)}, u32[]{:S(2)}) async-start(bf16[16,24,16,256]{3,2,1,0:T(8,128)(2,1)} %get-tuple-element.20), calls=%async_computation.2 | async-start | bytes 6291456 | tf_op jit(solution)/shard_map/all_to_all | solution.py:297
  116.1 20.9 %shard_map.88 = f32[4,72,256]{2,1,0:T(8,128)} custom-call(bf16[16,512,256]{2,1,0:T(8,128)(2,1)} %bitcast.25, f32[16,2,256]{2,1,0:T(2,128)} %maximum_convert_fusion.ends_ref, f32[3,256]{1,0:T(4,128)} %taps_ref.3, bf16[256,256]{1,0:T(8,128)(2,1)} %weight_ref.3, bf16[16,512,512]{2,1,0:T(8,128)(2,1)} %row_ref.3, bf16[16,8,16,256]{3,2,1,0:T(8,128)(2,1)} %all-to-all-done.refs_0_, ...), custom_call_target="tpu_custom_call" | custom-call | flops 4294967296 | bytes 16777216 | tf_op jit(solution)/shard_map/pallas_call | solution.py:274
  136.9 1.0 dynamic-slice_bitcast_fusion.2
  137.9 1.9 collective-permute-start.2
  139.8 1.5 collective-permute-start.4
  141.5 1.5 collective-permute-done.2
  143.0 16.1 %collective-permute-done.4 = f32[72,256]{1,0:T(8,128)S(1)} collective-permute-done((f32[72,256]{1,0:T(8,128)S(1)}, f32[72,256]{1,0:T(8,128)S(1)}, u32[]{:S(2)}, u32[]{:S(2)}) %collective-permute-start.4) | collective-permute-done | bytes 73760 | tf_op jit(solution)/shard_map/ppermute | solution.py:301
  159.0 0.9 fusion.1
  160.0 7.4 %collective-permute-done.5 = f32[72,256]{1,0:T(8,128)S(1)} collective-permute-done((f32[72,256]{1,0:T(8,128)S(1)}, f32[72,256]{1,0:T(8,128)S(1)}, u32[]{:S(2)}, u32[]{:S(2)}) %collective-permute-start.5) | collective-permute-done | bytes 73760 | tf_op jit(solution)/shard_map/ppermute | solution.py:301
  167.5 4.9 %collective-permute-start.6 = (f32[72,256]{1,0:T(8,128)S(1)}, f32[72,256]{1,0:T(8,128)S(1)}, u32[]{:S(2)}, u32[]{:S(2)}) collective-permute-start(f32[72,256]{1,0:T(8,128)S(1)} %add.41), channel_id=1, source_target_pairs={{0,16},{2,18},{4,20},{6,22},{8,24},{10,26},{12,28},{14,30},{16,0},... | collective-permute-start | bytes 221192 | tf_op jit(solution)/shard_map/ppermute | solution.py:301
  172.4 16.5 %collective-permute-done.6 = f32[72,256]{1,0:T(8,128)S(1)} collective-permute-done((f32[72,256]{1,0:T(8,128)S(1)}, f32[72,256]{1,0:T(8,128)S(1)}, u32[]{:S(2)}, u32[]{:S(2)}) %collective-permute-start.6) | collective-permute-done | bytes 73760 | tf_op jit(solution)/shard_map/ppermute | solution.py:301
  188.9 4.9 %all-to-all-start.3 = ((bf16[16,8,16,256]{3,2,1,0:T(8,128)(2,1)}), bf16[16,8,16,256]{3,2,1,0:T(8,128)(2,1)S(1)}, u32[]{:S(2)}, u32[]{:S(2)}) async-start(bf16[16,8,16,256]{3,2,1,0:T(8,128)(2,1)} %get-tuple-element.25), calls=%async_computation.3 | async-start | bytes 2097152 | tf_op jit(solution)/shard_map/all_to_all | solution.py:297
  193.9 1.3 slice.36.col
  195.2 2.0 collective-permute-start.9
  197.2 1.5 collective-permute-start.8
  198.7 4.6 %shard_map.89.before = bf16[32,256,256]{2,1,0:T(8,128)(2,1)} custom-call(bf16[32,256,256]{2,1,0:T(8,128)(2,1)} %col.5, bf16[16,24,16,256]{3,2,1,0:T(8,128)(2,1)} %all-to-all-done.2.recv), custom_call_target="tpu_custom_call" | custom-call | flops 805306368 | bytes 9437184 | tf_op jit(solution)/shard_map/pallas_call | solution.py:122
  203.8 2.8 %collective-permute-done.7 = f32[72,256]{1,0:T(8,128)S(1)} collective-permute-done((f32[72,256]{1,0:T(8,128)S(1)}, f32[72,256]{1,0:T(8,128)S(1)}, u32[]{:S(2)}, u32[]{:S(2)}) %collective-permute-start.7) | collective-permute-done | bytes 73760 | tf_op jit(solution)/shard_map/ppermute | solution.py:301
  207.3 0.7 pad_maximum_fusion
  208.1 8.4 %all-to-all-done.3.recv = bf16[16,8,16,256]{3,2,1,0:T(8,128)(2,1)S(1)} async-done(((bf16[16,8,16,256]{3,2,1,0:T(8,128)(2,1)}), bf16[16,8,16,256]{3,2,1,0:T(8,128)(2,1)S(1)}, u32[]{:S(2)}, u32[]{:S(2)}) %all-to-all-start.3) | async-done | bytes 1048608 | tf_op jit(solution)/shard_map/all_to_all | solution.py:297
  216.4 1.3 shard_map.90
  (25 shorter events, 1.6 us)
Async XLA Ops:
  3.4 32.9 %all-to-all-start = ((bf16[16,8,16,256]{3,2,1,0:T(8,128)(2,1)}), bf16[16,8,16,256]{3,2,1,0:T(8,128)(2,1)}, u32[]{:S(2)}, u32[]{:S(2)}) async-start(bf16[16,8,16,256]{3,2,1,0:T(8,128)(2,1)} %shard_map.86), calls=%async_computation | async-start | bytes 2097152 | tf_op jit(solution)/shard_map/all_to_all | solution.py:297
  12.5 10.3 %collective-permute-start.1 = (bf16[1,256]{1,0:T(2,128)(2,1)S(1)}, bf16[1,256]{1,0:T(2,128)(2,1)S(1)}, u32[]{:S(2)}, u32[]{:S(2)}) collective-permute-start(bf16[1,256]{1,0:T(2,128)(2,1)S(1)} %get-tuple-element.32), channel_id=1, source_target_pairs={{2,0},{4,2},{6,4},{8,6},{10,8},{12,10},{14,12},{16,14},{18,16},{20... | collective-permute-start | bytes 1544 | tf_op jit(solution)/shard_map/ppermute | solution.py:345
  13.8 9.0 %collective-permute-start = (bf16[1,256]{1,0:T(2,128)(2,1)S(1)}, bf16[1,256]{1,0:T(2,128)(2,1)S(1)}, u32[]{:S(2)}, u32[]{:S(2)}) collective-permute-start(bf16[1,256]{1,0:T(2,128)(2,1)S(1)} %get-tuple-element.33), channel_id=1, source_target_pairs={{0,2},{2,4},{4,6},{6,8},{8,10},{10,12},{12,14},{14,16},{16,18},{18... | collective-permute-start | bytes 1544 | tf_op jit(solution)/shard_map/ppermute | solution.py:344
  36.3 65.8 %all-to-all-start.1 = ((bf16[16,24,16,256]{3,2,1,0:T(8,128)(2,1)}), bf16[16,24,16,256]{3,2,1,0:T(8,128)(2,1)}, u32[]{:S(2)}, u32[]{:S(2)}) async-start(bf16[16,24,16,256]{3,2,1,0:T(8,128)(2,1)} %shard_map.85), calls=%async_computation.1 | async-start | bytes 6291456 | tf_op jit(solution)/shard_map/all_to_all | solution.py:297
  102.0 86.9 %all-to-all-start.2 = ((bf16[16,24,16,256]{3,2,1,0:T(8,128)(2,1)}), bf16[16,24,16,256]{3,2,1,0:T(8,128)(2,1)}, u32[]{:S(2)}, u32[]{:S(2)}) async-start(bf16[16,24,16,256]{3,2,1,0:T(8,128)(2,1)} %get-tuple-element.20), calls=%async_computation.2 | async-start | bytes 6291456 | tf_op jit(solution)/shard_map/all_to_all | solution.py:297
  137.9 5.1 %collective-permute-start.2 = (f32[72,256]{1,0:T(8,128)S(1)}, f32[72,256]{1,0:T(8,128)S(1)}, u32[]{:S(2)}, u32[]{:S(2)}) collective-permute-start(f32[72,256]{1,0:T(8,128)S(1)} %get-tuple-element.36), channel_id=1, source_target_pairs={{0,2},{2,0},{4,6},{6,4},{8,10},{10,8},{12,14},{14,12},{16,18},{18,... | collective-permute-start | bytes 221192 | tf_op jit(solution)/shard_map/ppermute | solution.py:301
  139.8 19.2 %collective-permute-start.4 = (f32[72,256]{1,0:T(8,128)S(1)}, f32[72,256]{1,0:T(8,128)S(1)}, u32[]{:S(2)}, u32[]{:S(2)}) collective-permute-start(f32[72,256]{1,0:T(8,128)S(1)} %get-tuple-element.37), channel_id=1, source_target_pairs={{0,6},{2,4},{4,2},{6,0},{8,14},{10,12},{12,10},{14,8},{16,22},{18,... | collective-permute-start | bytes 221192 | tf_op jit(solution)/shard_map/ppermute | solution.py:301
  141.3 17.8 %collective-permute-start.3 = (f32[72,256]{1,0:T(8,128)S(1)}, f32[72,256]{1,0:T(8,128)S(1)}, u32[]{:S(2)}, u32[]{:S(2)}) collective-permute-start(f32[72,256]{1,0:T(8,128)S(1)} %get-tuple-element.38), channel_id=1, source_target_pairs={{0,4},{2,6},{4,0},{6,2},{8,12},{10,14},{12,8},{14,10},{16,20},{18,... | collective-permute-start | bytes 221192 | tf_op jit(solution)/shard_map/ppermute | solution.py:301
  159.9 7.5 %collective-permute-start.5 = (f32[72,256]{1,0:T(8,128)S(1)}, f32[72,256]{1,0:T(8,128)S(1)}, u32[]{:S(2)}, u32[]{:S(2)}) collective-permute-start(f32[72,256]{1,0:T(8,128)S(1)} %fusion.1), channel_id=1, source_target_pairs={{0,8},{2,10},{4,12},{6,14},{8,0},{10,2},{12,4},{14,6},{16,24},{18,... | collective-permute-start | bytes 221192 | tf_op jit(solution)/shard_map/ppermute | solution.py:301
  167.5 21.4 %collective-permute-start.6 = (f32[72,256]{1,0:T(8,128)S(1)}, f32[72,256]{1,0:T(8,128)S(1)}, u32[]{:S(2)}, u32[]{:S(2)}) collective-permute-start(f32[72,256]{1,0:T(8,128)S(1)} %add.41), channel_id=1, source_target_pairs={{0,16},{2,18},{4,20},{6,22},{8,24},{10,26},{12,28},{14,30},{16,0},... | collective-permute-start | bytes 221192 | tf_op jit(solution)/shard_map/ppermute | solution.py:301
  188.9 27.5 %all-to-all-start.3 = ((bf16[16,8,16,256]{3,2,1,0:T(8,128)(2,1)}), bf16[16,8,16,256]{3,2,1,0:T(8,128)(2,1)S(1)}, u32[]{:S(2)}, u32[]{:S(2)}) async-start(bf16[16,8,16,256]{3,2,1,0:T(8,128)(2,1)} %get-tuple-element.25), calls=%async_computation.3 | async-start | bytes 2097152 | tf_op jit(solution)/shard_map/all_to_all | solution.py:297
  195.2 8.2 %collective-permute-start.9 = (f32[72,256]{1,0:T(8,128)S(1)}, f32[72,256]{1,0:T(8,128)S(1)}, u32[]{:S(2)}, u32[]{:S(2)}) collective-permute-start(f32[72,256]{1,0:T(8,128)S(1)} %add.42), channel_id=1, source_target_pairs={{0,2},{2,0},{4,6},{6,4},{8,10},{10,8},{12,14},{14,12},{16,18},{18,... | collective-permute-start | bytes 221192 | tf_op jit(solution)/shard_map/ppermute | solution.py:301
  197.2 6.7 %collective-permute-start.8 = (f32[72,256]{1,0:T(8,128)S(1)}, f32[72,256]{1,0:T(8,128)S(1)}, u32[]{:S(2)}, u32[]{:S(2)}) collective-permute-start(f32[72,256]{1,0:T(8,128)S(1)} %add.42), channel_id=1, source_target_pairs={{0,4},{2,6},{4,0},{6,2},{8,12},{10,14},{12,8},{14,10},{16,20},{18,... | collective-permute-start | bytes 221192 | tf_op jit(solution)/shard_map/ppermute | solution.py:301
  198.6 8.0 %collective-permute-start.7 = (f32[72,256]{1,0:T(8,128)S(1)}, f32[72,256]{1,0:T(8,128)S(1)}, u32[]{:S(2)}, u32[]{:S(2)}) collective-permute-start(f32[72,256]{1,0:T(8,128)S(1)} %add.42), channel_id=1, source_target_pairs={{0,6},{2,4},{4,2},{6,0},{8,14},{10,12},{12,10},{14,8},{16,22},{18,... | collective-permute-start | bytes 221192 | tf_op jit(solution)/shard_map/ppermute | solution.py:301

commit v6 on v5

--- a/solution.py
+++ b/solution.py
@@ -68,9 +68,10 @@
     _, order, runs_all = col.shape
     width = cot.shape[2]
     shape = (peers, count, runs_all // peers, width)
-    steps = count // GROUP
-    return pl.pallas_call(
-        functools.partial(back_first_kernel, peers, GROUP, start),
+    group = GROUP if start else max(1, GROUP // 2)
+    steps = count // group
+    return pl.pallas_call(
+        functools.partial(back_first_kernel, peers, group, start),
         in_specs=[pl.BlockSpec(memory_space=pl.ANY)] * 2,
         out_specs=pl.BlockSpec(memory_space=pl.ANY),
         out_shape=jax.ShapeDtypeStruct(shape, BF16),

time: 219 us -> 219 us (level)
  no operation moved by 1% of the time
where the time goes in v6:
time: 219 us; the launch traced here: 218 us
  waiting for transfers between devices  106 us (48%)
  Pallas kernels  53.1 us (24%)
  starting transfers between devices  51.1 us (23%)
  local copies, waits for them, and re-layouts  3.94 us (2%)
  other arithmetic  2.96 us (1%)
    all_to_all x4, waiting for transfers between devices, exchange(): return lax.all_to_all(block, 'ctx', split_axis=0, concat_axis=0, tiled=True)  61.1 us
    ppermute x8, waiting for transfers between devices, swapped(): return lax.ppermute(value, 'ctx', [(i, i ^ step) for i in range(peers)])  44.8 us
    all_to_all x4, starting transfers between devices, exchange(): return lax.all_to_all(block, 'ctx', split_axis=0, concat_axis=0, tiled=True)  33.2 us
    pallas_call x1, Pallas kernels, gradient_share(): pl.pallas_call(functools.partial(gradient_kernel, starts), grid=(runs,),...  20.9 us
    pallas_call x1, Pallas kernels, first_parts(): pl.pallas_call(functools.partial(first_kernel, peers, starts), grid=(runs...  19 us
    ppermute x8, starting transfers between devices, swapped(): return lax.ppermute(value, 'ctx', [(i, i ^ step) for i in range(peers)])  12.1 us
    pallas_call x2, Pallas kernels, back_first_part(): pl.pallas_call(functools.partial(back_first_kernel, peers, group, start),...  7.41 us
    pallas_call x1, Pallas kernels, mixed_part(): pl.pallas_call(functools.partial(mixed_kernel, GROUP, start), in_specs=[p...  4.59 us
  transfers between devices with their start and end apart: 14, of which 9 were waited for; matrix products, arithmetic and copies ran while one was open for 3% of the time, Pallas kernels for 22%

profile of v6, /device:TPU:0, one launch (start us, length us, event | category | flops | bytes accessed | tf_op | source)
XLA Modules:
  0.0 217.9 jit_solution(13752588253143829346)
XLA Ops:
  0.6 2.9 %shard_map.86 = bf16[16,8,16,256]{3,2,1,0:T(8,128)(2,1)} custom-call(bf16[32,256,256]{2,1,0:T(8,128)(2,1)} %col.5, bf16[32,256,256]{2,1,0:T(8,128)(2,1)} %cot.3), custom_call_target="tpu_custom_call" | custom-call | flops 268435456 | bytes 3145728 | tf_op jit(solution)/shard_map/pallas_call | solution.py:73
  3.6 8.4 %all-to-all-start = ((bf16[16,8,16,256]{3,2,1,0:T(8,128)(2,1)}), bf16[16,8,16,256]{3,2,1,0:T(8,128)(2,1)}, u32[]{:S(2)}, u32[]{:S(2)}) async-start(bf16[16,8,16,256]{3,2,1,0:T(8,128)(2,1)} %shard_map.86), calls=%async_computation | async-start | bytes 2097152 | tf_op jit(solution)/shard_map/all_to_all | solution.py:298
  12.0 0.7 fusion.3
  12.7 1.3 collective-permute-start.1
  14.0 4.5 %collective-permute-start = (bf16[1,256]{1,0:T(2,128)(2,1)S(1)}, bf16[1,256]{1,0:T(2,128)(2,1)S(1)}, u32[]{:S(2)}, u32[]{:S(2)}) collective-permute-start(bf16[1,256]{1,0:T(2,128)(2,1)S(1)} %get-tuple-element.33), channel_id=1, source_target_pairs={{0,2},{2,4},{4,6},{6,8},{8,10},{10,12},{12,14},{14,16},{16,18},{18... | collective-permute-start | bytes 1544 | tf_op jit(solution)/shard_map/ppermute | solution.py:345
  18.5 4.5 %shard_map.85 = bf16[16,24,16,256]{3,2,1,0:T(8,128)(2,1)} custom-call(bf16[32,256,256]{2,1,0:T(8,128)(2,1)} %col.5, bf16[32,256,256]{2,1,0:T(8,128)(2,1)} %cot.3), custom_call_target="tpu_custom_call" | custom-call | flops 805306368 | bytes 9437184 | tf_op jit(solution)/shard_map/pallas_call | solution.py:73
  23.0 13.4 %all-to-all-done.refs_0_ = bf16[16,8,16,256]{3,2,1,0:T(8,128)(2,1)} async-done(((bf16[16,8,16,256]{3,2,1,0:T(8,128)(2,1)}), bf16[16,8,16,256]{3,2,1,0:T(8,128)(2,1)}, u32[]{:S(2)}, u32[]{:S(2)}) %all-to-all-start) | async-done | bytes 1048608 | tf_op jit(solution)/shard_map/all_to_all | solution.py:298
  36.5 5.9 %all-to-all-start.1 = ((bf16[16,24,16,256]{3,2,1,0:T(8,128)(2,1)}), bf16[16,24,16,256]{3,2,1,0:T(8,128)(2,1)}, u32[]{:S(2)}, u32[]{:S(2)}) async-start(bf16[16,24,16,256]{3,2,1,0:T(8,128)(2,1)} %shard_map.85), calls=%async_computation.1 | async-start | bytes 6291456 | tf_op jit(solution)/shard_map/all_to_all | solution.py:298
  42.3 0.9 fusion.2
  43.3 0.7 maximum_convert_fusion.ends_ref
  44.0 19.0 %shard_map.87 = (bf16[16,24,16,256]{3,2,1,0:T(8,128)(2,1)}, bf16[16,8,16,256]{3,2,1,0:T(8,128)(2,1)}) custom-call(bf16[16,512,256]{2,1,0:T(8,128)(2,1)} %bitcast.24, f32[16,2,256]{2,1,0:T(2,128)} %maximum_convert_fusion.ends_ref, f32[3,256]{1,0:T(4,128)} %taps_ref.3, bf16[256,256]{1,0:T(8,128)(2,1)} %weight_ref.3, bf16[16,512,512]{2,1,0:T(8,128)(2,1)} %row_ref.3), custom_call_target="tpu_custom_call" | custom-call | flops 3221225472 | bytes 16777216 | tf_op jit(solution)/shard_map/pallas_call | solution.py:220
  63.0 39.3 %all-to-all-done.1.refs_1_ = bf16[16,24,16,256]{3,2,1,0:T(8,128)(2,1)} async-done(((bf16[16,24,16,256]{3,2,1,0:T(8,128)(2,1)}), bf16[16,24,16,256]{3,2,1,0:T(8,128)(2,1)}, u32[]{:S(2)}, u32[]{:S(2)}) %all-to-all-start.1) | async-done | bytes 3145760 | tf_op jit(solution)/shard_map/all_to_all | solution.py:298
  102.2 14.0 %all-to-all-start.2 = ((bf16[16,24,16,256]{3,2,1,0:T(8,128)(2,1)}), bf16[16,24,16,256]{3,2,1,0:T(8,128)(2,1)}, u32[]{:S(2)}, u32[]{:S(2)}) async-start(bf16[16,24,16,256]{3,2,1,0:T(8,128)(2,1)} %get-tuple-element.20), calls=%async_computation.2 | async-start | bytes 6291456 | tf_op jit(solution)/shard_map/all_to_all | solution.py:298
  116.3 20.9 %shard_map.88 = f32[4,72,256]{2,1,0:T(8,128)} custom-call(bf16[16,512,256]{2,1,0:T(8,128)(2,1)} %bitcast.25, f32[16,2,256]{2,1,0:T(2,128)} %maximum_convert_fusion.ends_ref, f32[3,256]{1,0:T(4,128)} %taps_ref.3, bf16[256,256]{1,0:T(8,128)(2,1)} %weight_ref.3, bf16[16,512,512]{2,1,0:T(8,128)(2,1)} %row_ref.3, bf16[16,8,16,256]{3,2,1,0:T(8,128)(2,1)} %all-to-all-done.refs_0_, ...), custom_call_target="tpu_custom_call" | custom-call | flops 4294967296 | bytes 16777216 | tf_op jit(solution)/shard_map/pallas_call | solution.py:275
  137.1 1.0 dynamic-slice_bitcast_fusion.2
  138.1 1.9 collective-permute-start.2
  140.0 1.5 collective-permute-start.4
  141.7 1.5 collective-permute-done.2
  143.2 16.1 %collective-permute-done.4 = f32[72,256]{1,0:T(8,128)S(1)} collective-permute-done((f32[72,256]{1,0:T(8,128)S(1)}, f32[72,256]{1,0:T(8,128)S(1)}, u32[]{:S(2)}, u32[]{:S(2)}) %collective-permute-start.4) | collective-permute-done | bytes 73760 | tf_op jit(solution)/shard_map/ppermute | solution.py:302
  159.2 0.9 fusion.1
  160.2 7.4 %collective-permute-done.5 = f32[72,256]{1,0:T(8,128)S(1)} collective-permute-done((f32[72,256]{1,0:T(8,128)S(1)}, f32[72,256]{1,0:T(8,128)S(1)}, u32[]{:S(2)}, u32[]{:S(2)}) %collective-permute-start.5) | collective-permute-done | bytes 73760 | tf_op jit(solution)/shard_map/ppermute | solution.py:302
  167.7 4.9 %collective-permute-start.6 = (f32[72,256]{1,0:T(8,128)S(1)}, f32[72,256]{1,0:T(8,128)S(1)}, u32[]{:S(2)}, u32[]{:S(2)}) collective-permute-start(f32[72,256]{1,0:T(8,128)S(1)} %add.41), channel_id=1, source_target_pairs={{0,16},{2,18},{4,20},{6,22},{8,24},{10,26},{12,28},{14,30},{16,0},... | collective-permute-start | bytes 221192 | tf_op jit(solution)/shard_map/ppermute | solution.py:302
  172.6 16.5 %collective-permute-done.6 = f32[72,256]{1,0:T(8,128)S(1)} collective-permute-done((f32[72,256]{1,0:T(8,128)S(1)}, f32[72,256]{1,0:T(8,128)S(1)}, u32[]{:S(2)}, u32[]{:S(2)}) %collective-permute-start.6) | collective-permute-done | bytes 73760 | tf_op jit(solution)/shard_map/ppermute | solution.py:302
  189.1 4.9 %all-to-all-start.3 = ((bf16[16,8,16,256]{3,2,1,0:T(8,128)(2,1)}), bf16[16,8,16,256]{3,2,1,0:T(8,128)(2,1)S(1)}, u32[]{:S(2)}, u32[]{:S(2)}) async-start(bf16[16,8,16,256]{3,2,1,0:T(8,128)(2,1)} %get-tuple-element.25), calls=%async_computation.3 | async-start | bytes 2097152 | tf_op jit(solution)/shard_map/all_to_all | solution.py:298
  194.1 1.3 slice.36.col
  195.4 2.0 collective-permute-start.9
  197.3 1.5 collective-permute-start.8
  198.9 4.6 %shard_map.89.before = bf16[32,256,256]{2,1,0:T(8,128)(2,1)} custom-call(bf16[32,256,256]{2,1,0:T(8,128)(2,1)} %col.5, bf16[16,24,16,256]{3,2,1,0:T(8,128)(2,1)} %all-to-all-done.2.recv), custom_call_target="tpu_custom_call" | custom-call | flops 805306368 | bytes 9437184 | tf_op jit(solution)/shard_map/pallas_call | solution.py:123
  204.0 2.8 %collective-permute-done.7 = f32[72,256]{1,0:T(8,128)S(1)} collective-permute-done((f32[72,256]{1,0:T(8,128)S(1)}, f32[72,256]{1,0:T(8,128)S(1)}, u32[]{:S(2)}, u32[]{:S(2)}) %collective-permute-start.7) | collective-permute-done | bytes 73760 | tf_op jit(solution)/shard_map/ppermute | solution.py:302
  207.5 0.7 pad_maximum_fusion
  208.3 8.4 %all-to-all-done.3.recv = bf16[16,8,16,256]{3,2,1,0:T(8,128)(2,1)S(1)} async-done(((bf16[16,8,16,256]{3,2,1,0:T(8,128)(2,1)}), bf16[16,8,16,256]{3,2,1,0:T(8,128)(2,1)S(1)}, u32[]{:S(2)}, u32[]{:S(2)}) %all-to-all-start.3) | async-done | bytes 1048608 | tf_op jit(solution)/shard_map/all_to_all | solution.py:298
  216.6 1.3 shard_map.90
  (25 shorter events, 1.6 us)
Async XLA Ops:
  3.6 32.9 %all-to-all-start = ((bf16[16,8,16,256]{3,2,1,0:T(8,128)(2,1)}), bf16[16,8,16,256]{3,2,1,0:T(8,128)(2,1)}, u32[]{:S(2)}, u32[]{:S(2)}) async-start(bf16[16,8,16,256]{3,2,1,0:T(8,128)(2,1)} %shard_map.86), calls=%async_computation | async-start | bytes 2097152 | tf_op jit(solution)/shard_map/all_to_all | solution.py:298
  12.7 10.3 %collective-permute-start.1 = (bf16[1,256]{1,0:T(2,128)(2,1)S(1)}, bf16[1,256]{1,0:T(2,128)(2,1)S(1)}, u32[]{:S(2)}, u32[]{:S(2)}) collective-permute-start(bf16[1,256]{1,0:T(2,128)(2,1)S(1)} %get-tuple-element.32), channel_id=1, source_target_pairs={{2,0},{4,2},{6,4},{8,6},{10,8},{12,10},{14,12},{16,14},{18,16},{20... | collective-permute-start | bytes 1544 | tf_op jit(solution)/shard_map/ppermute | solution.py:346
  14.0 9.0 %collective-permute-start = (bf16[1,256]{1,0:T(2,128)(2,1)S(1)}, bf16[1,256]{1,0:T(2,128)(2,1)S(1)}, u32[]{:S(2)}, u32[]{:S(2)}) collective-permute-start(bf16[1,256]{1,0:T(2,128)(2,1)S(1)} %get-tuple-element.33), channel_id=1, source_target_pairs={{0,2},{2,4},{4,6},{6,8},{8,10},{10,12},{12,14},{14,16},{16,18},{18... | collective-permute-start | bytes 1544 | tf_op jit(solution)/shard_map/ppermute | solution.py:345
  36.5 65.8 %all-to-all-start.1 = ((bf16[16,24,16,256]{3,2,1,0:T(8,128)(2,1)}), bf16[16,24,16,256]{3,2,1,0:T(8,128)(2,1)}, u32[]{:S(2)}, u32[]{:S(2)}) async-start(bf16[16,24,16,256]{3,2,1,0:T(8,128)(2,1)} %shard_map.85), calls=%async_computation.1 | async-start | bytes 6291456 | tf_op jit(solution)/shard_map/all_to_all | solution.py:298
  102.2 86.9 %all-to-all-start.2 = ((bf16[16,24,16,256]{3,2,1,0:T(8,128)(2,1)}), bf16[16,24,16,256]{3,2,1,0:T(8,128)(2,1)}, u32[]{:S(2)}, u32[]{:S(2)}) async-start(bf16[16,24,16,256]{3,2,1,0:T(8,128)(2,1)} %get-tuple-element.20), calls=%async_computation.2 | async-start | bytes 6291456 | tf_op jit(solution)/shard_map/all_to_all | solution.py:298
  138.1 5.1 %collective-permute-start.2 = (f32[72,256]{1,0:T(8,128)S(1)}, f32[72,256]{1,0:T(8,128)S(1)}, u32[]{:S(2)}, u32[]{:S(2)}) collective-permute-start(f32[72,256]{1,0:T(8,128)S(1)} %get-tuple-element.36), channel_id=1, source_target_pairs={{0,2},{2,0},{4,6},{6,4},{8,10},{10,8},{12,14},{14,12},{16,18},{18,... | collective-permute-start | bytes 221192 | tf_op jit(solution)/shard_map/ppermute | solution.py:302
  140.0 19.2 %collective-permute-start.4 = (f32[72,256]{1,0:T(8,128)S(1)}, f32[72,256]{1,0:T(8,128)S(1)}, u32[]{:S(2)}, u32[]{:S(2)}) collective-permute-start(f32[72,256]{1,0:T(8,128)S(1)} %get-tuple-element.37), channel_id=1, source_target_pairs={{0,6},{2,4},{4,2},{6,0},{8,14},{10,12},{12,10},{14,8},{16,22},{18,... | collective-permute-start | bytes 221192 | tf_op jit(solution)/shard_map/ppermute | solution.py:302
  141.5 17.8 %collective-permute-start.3 = (f32[72,256]{1,0:T(8,128)S(1)}, f32[72,256]{1,0:T(8,128)S(1)}, u32[]{:S(2)}, u32[]{:S(2)}) collective-permute-start(f32[72,256]{1,0:T(8,128)S(1)} %get-tuple-element.38), channel_id=1, source_target_pairs={{0,4},{2,6},{4,0},{6,2},{8,12},{10,14},{12,8},{14,10},{16,20},{18,... | collective-permute-start | bytes 221192 | tf_op jit(solution)/shard_map/ppermute | solution.py:302
  160.1 7.5 %collective-permute-start.5 = (f32[72,256]{1,0:T(8,128)S(1)}, f32[72,256]{1,0:T(8,128)S(1)}, u32[]{:S(2)}, u32[]{:S(2)}) collective-permute-start(f32[72,256]{1,0:T(8,128)S(1)} %fusion.1), channel_id=1, source_target_pairs={{0,8},{2,10},{4,12},{6,14},{8,0},{10,2},{12,4},{14,6},{16,24},{18,... | collective-permute-start | bytes 221192 | tf_op jit(solution)/shard_map/ppermute | solution.py:302
  167.7 21.4 %collective-permute-start.6 = (f32[72,256]{1,0:T(8,128)S(1)}, f32[72,256]{1,0:T(8,128)S(1)}, u32[]{:S(2)}, u32[]{:S(2)}) collective-permute-start(f32[72,256]{1,0:T(8,128)S(1)} %add.41), channel_id=1, source_target_pairs={{0,16},{2,18},{4,20},{6,22},{8,24},{10,26},{12,28},{14,30},{16,0},... | collective-permute-start | bytes 221192 | tf_op jit(solution)/shard_map/ppermute | solution.py:302
  189.1 27.5 %all-to-all-start.3 = ((bf16[16,8,16,256]{3,2,1,0:T(8,128)(2,1)}), bf16[16,8,16,256]{3,2,1,0:T(8,128)(2,1)S(1)}, u32[]{:S(2)}, u32[]{:S(2)}) async-start(bf16[16,8,16,256]{3,2,1,0:T(8,128)(2,1)} %get-tuple-element.25), calls=%async_computation.3 | async-start | bytes 2097152 | tf_op jit(solution)/shard_map/all_to_all | solution.py:298
  195.4 8.2 %collective-permute-start.9 = (f32[72,256]{1,0:T(8,128)S(1)}, f32[72,256]{1,0:T(8,128)S(1)}, u32[]{:S(2)}, u32[]{:S(2)}) collective-permute-start(f32[72,256]{1,0:T(8,128)S(1)} %add.42), channel_id=1, source_target_pairs={{0,2},{2,0},{4,6},{6,4},{8,10},{10,8},{12,14},{14,12},{16,18},{18,... | collective-permute-start | bytes 221192 | tf_op jit(solution)/shard_map/ppermute | solution.py:302
  197.3 6.7 %collective-permute-start.8 = (f32[72,256]{1,0:T(8,128)S(1)}, f32[72,256]{1,0:T(8,128)S(1)}, u32[]{:S(2)}, u32[]{:S(2)}) collective-permute-start(f32[72,256]{1,0:T(8,128)S(1)} %add.42), channel_id=1, source_target_pairs={{0,4},{2,6},{4,0},{6,2},{8,12},{10,14},{12,8},{14,10},{16,20},{18,... | collective-permute-start | bytes 221192 | tf_op jit(solution)/shard_map/ppermute | solution.py:302
  198.8 8.0 %collective-permute-start.7 = (f32[72,256]{1,0:T(8,128)S(1)}, f32[72,256]{1,0:T(8,128)S(1)}, u32[]{:S(2)}, u32[]{:S(2)}) collective-permute-start(f32[72,256]{1,0:T(8,128)S(1)} %add.42), channel_id=1, source_target_pairs={{0,6},{2,4},{4,2},{6,0},{8,14},{10,12},{12,10},{14,8},{16,22},{18,... | collective-permute-start | bytes 221192 | tf_op jit(solution)/shard_map/ppermute | solution.py:302

commit v7 on v6

--- a/solution.py
+++ b/solution.py
@@ -157,10 +157,10 @@
 def last_mixed_part(col, recv, start, before):
     count, order, runs_all = col.shape
     width = recv.shape[3]
-    steps = count // GROUP
+    steps = count // (GROUP // 2)
     vmem = pl.BlockSpec(memory_space=pltpu.VMEM)
     return pl.pallas_call(
-        functools.partial(last_mixed_kernel, GROUP, start),
+        functools.partial(last_mixed_kernel, GROUP // 2, start),
         in_specs=[vmem, vmem, pl.BlockSpec(memory_space=pl.ANY)],
         out_specs=pl.BlockSpec(memory_space=pl.ANY),
         out_shape=jax.ShapeDtypeStruct(before.shape, BF16),

time: 219 us -> 219 us (level)
  no operation moved by 1% of the time
where the time goes in v7:
time: 219 us; the launch traced here: 218 us
  waiting for transfers between devices  106 us (48%)
  Pallas kernels  53.1 us (24%)
  starting transfers between devices  51.1 us (23%)
  local copies, waits for them, and re-layouts  3.94 us (2%)
  other arithmetic  2.96 us (1%)
    all_to_all x4, waiting for transfers between devices, exchange(): return lax.all_to_all(block, 'ctx', split_axis=0, concat_axis=0, tiled=True)  61.1 us
    ppermute x8, waiting for transfers between devices, swapped(): return lax.ppermute(value, 'ctx', [(i, i ^ step) for i in range(peers)])  44.8 us
    all_to_all x4, starting transfers between devices, exchange(): return lax.all_to_all(block, 'ctx', split_axis=0, concat_axis=0, tiled=True)  33.2 us
    pallas_call x1, Pallas kernels, gradient_share(): pl.pallas_call(functools.partial(gradient_kernel, starts), grid=(runs,),...  20.9 us
    pallas_call x1, Pallas kernels, first_parts(): pl.pallas_call(functools.partial(first_kernel, peers, starts), grid=(runs...  19 us
    ppermute x8, starting transfers between devices, swapped(): return lax.ppermute(value, 'ctx', [(i, i ^ step) for i in range(peers)])  12.1 us
    pallas_call x2, Pallas kernels, back_first_part(): pl.pallas_call(functools.partial(back_first_kernel, peers, group, start),...  7.41 us
    pallas_call x1, Pallas kernels, mixed_part(): pl.pallas_call(functools.partial(mixed_kernel, GROUP, start), in_specs=[p...  4.59 us
  transfers between devices with their start and end apart: 14, of which 9 were waited for; matrix products, arithmetic and copies ran while one was open for 3% of the time, Pallas kernels for 22%

profile of v7, /device:TPU:0, one launch (start us, length us, event | category | flops | bytes accessed | tf_op | source)
XLA Modules:
  0.0 217.9 jit_solution(13789784089809387054)
XLA Ops:
  0.6 2.9 %shard_map.86 = bf16[16,8,16,256]{3,2,1,0:T(8,128)(2,1)} custom-call(bf16[32,256,256]{2,1,0:T(8,128)(2,1)} %col.5, bf16[32,256,256]{2,1,0:T(8,128)(2,1)} %cot.3), custom_call_target="tpu_custom_call" | custom-call | flops 268435456 | bytes 3145728 | tf_op jit(solution)/shard_map/pallas_call | solution.py:73
  3.6 8.4 %all-to-all-start = ((bf16[16,8,16,256]{3,2,1,0:T(8,128)(2,1)}), bf16[16,8,16,256]{3,2,1,0:T(8,128)(2,1)}, u32[]{:S(2)}, u32[]{:S(2)}) async-start(bf16[16,8,16,256]{3,2,1,0:T(8,128)(2,1)} %shard_map.86), calls=%async_computation | async-start | bytes 2097152 | tf_op jit(solution)/shard_map/all_to_all | solution.py:298
  12.0 0.7 fusion.3
  12.7 1.3 collective-permute-start.1
  14.0 4.5 %collective-permute-start = (bf16[1,256]{1,0:T(2,128)(2,1)S(1)}, bf16[1,256]{1,0:T(2,128)(2,1)S(1)}, u32[]{:S(2)}, u32[]{:S(2)}) collective-permute-start(bf16[1,256]{1,0:T(2,128)(2,1)S(1)} %get-tuple-element.33), channel_id=1, source_target_pairs={{0,2},{2,4},{4,6},{6,8},{8,10},{10,12},{12,14},{14,16},{16,18},{18... | collective-permute-start | bytes 1544 | tf_op jit(solution)/shard_map/ppermute | solution.py:345
  18.5 4.5 %shard_map.85 = bf16[16,24,16,256]{3,2,1,0:T(8,128)(2,1)} custom-call(bf16[32,256,256]{2,1,0:T(8,128)(2,1)} %col.5, bf16[32,256,256]{2,1,0:T(8,128)(2,1)} %cot.3), custom_call_target="tpu_custom_call" | custom-call | flops 805306368 | bytes 9437184 | tf_op jit(solution)/shard_map/pallas_call | solution.py:73
  23.0 13.4 %all-to-all-done.refs_0_ = bf16[16,8,16,256]{3,2,1,0:T(8,128)(2,1)} async-done(((bf16[16,8,16,256]{3,2,1,0:T(8,128)(2,1)}), bf16[16,8,16,256]{3,2,1,0:T(8,128)(2,1)}, u32[]{:S(2)}, u32[]{:S(2)}) %all-to-all-start) | async-done | bytes 1048608 | tf_op jit(solution)/shard_map/all_to_all | solution.py:298
  36.5 5.9 %all-to-all-start.1 = ((bf16[16,24,16,256]{3,2,1,0:T(8,128)(2,1)}), bf16[16,24,16,256]{3,2,1,0:T(8,128)(2,1)}, u32[]{:S(2)}, u32[]{:S(2)}) async-start(bf16[16,24,16,256]{3,2,1,0:T(8,128)(2,1)} %shard_map.85), calls=%async_computation.1 | async-start | bytes 6291456 | tf_op jit(solution)/shard_map/all_to_all | solution.py:298
  42.3 0.9 fusion.2
  43.3 0.7 maximum_convert_fusion.ends_ref
  44.0 19.0 %shard_map.87 = (bf16[16,24,16,256]{3,2,1,0:T(8,128)(2,1)}, bf16[16,8,16,256]{3,2,1,0:T(8,128)(2,1)}) custom-call(bf16[16,512,256]{2,1,0:T(8,128)(2,1)} %bitcast.24, f32[16,2,256]{2,1,0:T(2,128)} %maximum_convert_fusion.ends_ref, f32[3,256]{1,0:T(4,128)} %taps_ref.3, bf16[256,256]{1,0:T(8,128)(2,1)} %weight_ref.3, bf16[16,512,512]{2,1,0:T(8,128)(2,1)} %row_ref.3), custom_call_target="tpu_custom_call" | custom-call | flops 3221225472 | bytes 16777216 | tf_op jit(solution)/shard_map/pallas_call | solution.py:220
  63.0 39.3 %all-to-all-done.1.refs_1_ = bf16[16,24,16,256]{3,2,1,0:T(8,128)(2,1)} async-done(((bf16[16,24,16,256]{3,2,1,0:T(8,128)(2,1)}), bf16[16,24,16,256]{3,2,1,0:T(8,128)(2,1)}, u32[]{:S(2)}, u32[]{:S(2)}) %all-to-all-start.1) | async-done | bytes 3145760 | tf_op jit(solution)/shard_map/all_to_all | solution.py:298
  102.2 14.0 %all-to-all-start.2 = ((bf16[16,24,16,256]{3,2,1,0:T(8,128)(2,1)}), bf16[16,24,16,256]{3,2,1,0:T(8,128)(2,1)}, u32[]{:S(2)}, u32[]{:S(2)}) async-start(bf16[16,24,16,256]{3,2,1,0:T(8,128)(2,1)} %get-tuple-element.20), calls=%async_computation.2 | async-start | bytes 6291456 | tf_op jit(solution)/shard_map/all_to_all | solution.py:298
  116.3 20.9 %shard_map.88 = f32[4,72,256]{2,1,0:T(8,128)} custom-call(bf16[16,512,256]{2,1,0:T(8,128)(2,1)} %bitcast.25, f32[16,2,256]{2,1,0:T(2,128)} %maximum_convert_fusion.ends_ref, f32[3,256]{1,0:T(4,128)} %taps_ref.3, bf16[256,256]{1,0:T(8,128)(2,1)} %weight_ref.3, bf16[16,512,512]{2,1,0:T(8,128)(2,1)} %row_ref.3, bf16[16,8,16,256]{3,2,1,0:T(8,128)(2,1)} %all-to-all-done.refs_0_, ...), custom_call_target="tpu_custom_call" | custom-call | flops 4294967296 | bytes 16777216 | tf_op jit(solution)/shard_map/pallas_call | solution.py:275
  137.1 1.0 dynamic-slice_bitcast_fusion.2
  138.1 1.9 collective-permute-start.2
  140.0 1.5 collective-permute-start.4
  141.7 1.5 collective-permute-done.2
  143.2 16.1 %collective-permute-done.4 = f32[72,256]{1,0:T(8,128)S(1)} collective-permute-done((f32[72,256]{1,0:T(8,128)S(1)}, f32[72,256]{1,0:T(8,128)S(1)}, u32[]{:S(2)}, u32[]{:S(2)}) %collective-permute-start.4) | collective-permute-done | bytes 73760 | tf_op jit(solution)/shard_map/ppermute | solution.py:302
  159.2 0.9 fusion.1
  160.2 7.4 %collective-permute-done.5 = f32[72,256]{1,0:T(8,128)S(1)} collective-permute-done((f32[72,256]{1,0:T(8,128)S(1)}, f32[72,256]{1,0:T(8,128)S(1)}, u32[]{:S(2)}, u32[]{:S(2)}) %collective-permute-start.5) | collective-permute-done | bytes 73760 | tf_op jit(solution)/shard_map/ppermute | solution.py:302
  167.7 4.9 %collective-permute-start.6 = (f32[72,256]{1,0:T(8,128)S(1)}, f32[72,256]{1,0:T(8,128)S(1)}, u32[]{:S(2)}, u32[]{:S(2)}) collective-permute-start(f32[72,256]{1,0:T(8,128)S(1)} %add.41), channel_id=1, source_target_pairs={{0,16},{2,18},{4,20},{6,22},{8,24},{10,26},{12,28},{14,30},{16,0},... | collective-permute-start | bytes 221192 | tf_op jit(solution)/shard_map/ppermute | solution.py:302
  172.6 16.5 %collective-permute-done.6 = f32[72,256]{1,0:T(8,128)S(1)} collective-permute-done((f32[72,256]{1,0:T(8,128)S(1)}, f32[72,256]{1,0:T(8,128)S(1)}, u32[]{:S(2)}, u32[]{:S(2)}) %collective-permute-start.6) | collective-permute-done | bytes 73760 | tf_op jit(solution)/shard_map/ppermute | solution.py:302
  189.1 4.9 %all-to-all-start.3 = ((bf16[16,8,16,256]{3,2,1,0:T(8,128)(2,1)}), bf16[16,8,16,256]{3,2,1,0:T(8,128)(2,1)S(1)}, u32[]{:S(2)}, u32[]{:S(2)}) async-start(bf16[16,8,16,256]{3,2,1,0:T(8,128)(2,1)} %get-tuple-element.25), calls=%async_computation.3 | async-start | bytes 2097152 | tf_op jit(solution)/shard_map/all_to_all | solution.py:298
  194.1 1.3 slice.36.col
  195.4 2.0 collective-permute-start.9
  197.3 1.5 collective-permute-start.8
  198.9 4.6 %shard_map.89.before = bf16[32,256,256]{2,1,0:T(8,128)(2,1)} custom-call(bf16[32,256,256]{2,1,0:T(8,128)(2,1)} %col.5, bf16[16,24,16,256]{3,2,1,0:T(8,128)(2,1)} %all-to-all-done.2.recv), custom_call_target="tpu_custom_call" | custom-call | flops 805306368 | bytes 9437184 | tf_op jit(solution)/shard_map/pallas_call | solution.py:123
  204.0 2.8 %collective-permute-done.7 = f32[72,256]{1,0:T(8,128)S(1)} collective-permute-done((f32[72,256]{1,0:T(8,128)S(1)}, f32[72,256]{1,0:T(8,128)S(1)}, u32[]{:S(2)}, u32[]{:S(2)}) %collective-permute-start.7) | collective-permute-done | bytes 73760 | tf_op jit(solution)/shard_map/ppermute | solution.py:302
  207.5 0.7 pad_maximum_fusion
  208.3 8.4 %all-to-all-done.3.recv = bf16[16,8,16,256]{3,2,1,0:T(8,128)(2,1)S(1)} async-done(((bf16[16,8,16,256]{3,2,1,0:T(8,128)(2,1)}), bf16[16,8,16,256]{3,2,1,0:T(8,128)(2,1)S(1)}, u32[]{:S(2)}, u32[]{:S(2)}) %all-to-all-start.3) | async-done | bytes 1048608 | tf_op jit(solution)/shard_map/all_to_all | solution.py:298
  216.6 1.2 shard_map.90
  (25 shorter events, 1.6 us)
Async XLA Ops:
  3.6 32.9 %all-to-all-start = ((bf16[16,8,16,256]{3,2,1,0:T(8,128)(2,1)}), bf16[16,8,16,256]{3,2,1,0:T(8,128)(2,1)}, u32[]{:S(2)}, u32[]{:S(2)}) async-start(bf16[16,8,16,256]{3,2,1,0:T(8,128)(2,1)} %shard_map.86), calls=%async_computation | async-start | bytes 2097152 | tf_op jit(solution)/shard_map/all_to_all | solution.py:298
  12.7 10.3 %collective-permute-start.1 = (bf16[1,256]{1,0:T(2,128)(2,1)S(1)}, bf16[1,256]{1,0:T(2,128)(2,1)S(1)}, u32[]{:S(2)}, u32[]{:S(2)}) collective-permute-start(bf16[1,256]{1,0:T(2,128)(2,1)S(1)} %get-tuple-element.32), channel_id=1, source_target_pairs={{2,0},{4,2},{6,4},{8,6},{10,8},{12,10},{14,12},{16,14},{18,16},{20... | collective-permute-start | bytes 1544 | tf_op jit(solution)/shard_map/ppermute | solution.py:346
  14.0 9.0 %collective-permute-start = (bf16[1,256]{1,0:T(2,128)(2,1)S(1)}, bf16[1,256]{1,0:T(2,128)(2,1)S(1)}, u32[]{:S(2)}, u32[]{:S(2)}) collective-permute-start(bf16[1,256]{1,0:T(2,128)(2,1)S(1)} %get-tuple-element.33), channel_id=1, source_target_pairs={{0,2},{2,4},{4,6},{6,8},{8,10},{10,12},{12,14},{14,16},{16,18},{18... | collective-permute-start | bytes 1544 | tf_op jit(solution)/shard_map/ppermute | solution.py:345
  36.5 65.8 %all-to-all-start.1 = ((bf16[16,24,16,256]{3,2,1,0:T(8,128)(2,1)}), bf16[16,24,16,256]{3,2,1,0:T(8,128)(2,1)}, u32[]{:S(2)}, u32[]{:S(2)}) async-start(bf16[16,24,16,256]{3,2,1,0:T(8,128)(2,1)} %shard_map.85), calls=%async_computation.1 | async-start | bytes 6291456 | tf_op jit(solution)/shard_map/all_to_all | solution.py:298
  102.2 86.9 %all-to-all-start.2 = ((bf16[16,24,16,256]{3,2,1,0:T(8,128)(2,1)}), bf16[16,24,16,256]{3,2,1,0:T(8,128)(2,1)}, u32[]{:S(2)}, u32[]{:S(2)}) async-start(bf16[16,24,16,256]{3,2,1,0:T(8,128)(2,1)} %get-tuple-element.20), calls=%async_computation.2 | async-start | bytes 6291456 | tf_op jit(solution)/shard_map/all_to_all | solution.py:298
  138.1 5.1 %collective-permute-start.2 = (f32[72,256]{1,0:T(8,128)S(1)}, f32[72,256]{1,0:T(8,128)S(1)}, u32[]{:S(2)}, u32[]{:S(2)}) collective-permute-start(f32[72,256]{1,0:T(8,128)S(1)} %get-tuple-element.36), channel_id=1, source_target_pairs={{0,2},{2,0},{4,6},{6,4},{8,10},{10,8},{12,14},{14,12},{16,18},{18,... | collective-permute-start | bytes 221192 | tf_op jit(solution)/shard_map/ppermute | solution.py:302
  140.0 19.2 %collective-permute-start.4 = (f32[72,256]{1,0:T(8,128)S(1)}, f32[72,256]{1,0:T(8,128)S(1)}, u32[]{:S(2)}, u32[]{:S(2)}) collective-permute-start(f32[72,256]{1,0:T(8,128)S(1)} %get-tuple-element.37), channel_id=1, source_target_pairs={{0,6},{2,4},{4,2},{6,0},{8,14},{10,12},{12,10},{14,8},{16,22},{18,... | collective-permute-start | bytes 221192 | tf_op jit(solution)/shard_map/ppermute | solution.py:302
  141.5 17.8 %collective-permute-start.3 = (f32[72,256]{1,0:T(8,128)S(1)}, f32[72,256]{1,0:T(8,128)S(1)}, u32[]{:S(2)}, u32[]{:S(2)}) collective-permute-start(f32[72,256]{1,0:T(8,128)S(1)} %get-tuple-element.38), channel_id=1, source_target_pairs={{0,4},{2,6},{4,0},{6,2},{8,12},{10,14},{12,8},{14,10},{16,20},{18,... | collective-permute-start | bytes 221192 | tf_op jit(solution)/shard_map/ppermute | solution.py:302
  160.1 7.5 %collective-permute-start.5 = (f32[72,256]{1,0:T(8,128)S(1)}, f32[72,256]{1,0:T(8,128)S(1)}, u32[]{:S(2)}, u32[]{:S(2)}) collective-permute-start(f32[72,256]{1,0:T(8,128)S(1)} %fusion.1), channel_id=1, source_target_pairs={{0,8},{2,10},{4,12},{6,14},{8,0},{10,2},{12,4},{14,6},{16,24},{18,... | collective-permute-start | bytes 221192 | tf_op jit(solution)/shard_map/ppermute | solution.py:302
  167.7 21.4 %collective-permute-start.6 = (f32[72,256]{1,0:T(8,128)S(1)}, f32[72,256]{1,0:T(8,128)S(1)}, u32[]{:S(2)}, u32[]{:S(2)}) collective-permute-start(f32[72,256]{1,0:T(8,128)S(1)} %add.41), channel_id=1, source_target_pairs={{0,16},{2,18},{4,20},{6,22},{8,24},{10,26},{12,28},{14,30},{16,0},... | collective-permute-start | bytes 221192 | tf_op jit(solution)/shard_map/ppermute | solution.py:302
  189.1 27.5 %all-to-all-start.3 = ((bf16[16,8,16,256]{3,2,1,0:T(8,128)(2,1)}), bf16[16,8,16,256]{3,2,1,0:T(8,128)(2,1)S(1)}, u32[]{:S(2)}, u32[]{:S(2)}) async-start(bf16[16,8,16,256]{3,2,1,0:T(8,128)(2,1)} %get-tuple-element.25), calls=%async_computation.3 | async-start | bytes 2097152 | tf_op jit(solution)/shard_map/all_to_all | solution.py:298
  195.4 8.2 %collective-permute-start.9 = (f32[72,256]{1,0:T(8,128)S(1)}, f32[72,256]{1,0:T(8,128)S(1)}, u32[]{:S(2)}, u32[]{:S(2)}) collective-permute-start(f32[72,256]{1,0:T(8,128)S(1)} %add.42), channel_id=1, source_target_pairs={{0,2},{2,0},{4,6},{6,4},{8,10},{10,8},{12,14},{14,12},{16,18},{18,... | collective-permute-start | bytes 221192 | tf_op jit(solution)/shard_map/ppermute | solution.py:302
  197.3 6.7 %collective-permute-start.8 = (f32[72,256]{1,0:T(8,128)S(1)}, f32[72,256]{1,0:T(8,128)S(1)}, u32[]{:S(2)}, u32[]{:S(2)}) collective-permute-start(f32[72,256]{1,0:T(8,128)S(1)} %add.42), channel_id=1, source_target_pairs={{0,4},{2,6},{4,0},{6,2},{8,12},{10,14},{12,8},{14,10},{16,20},{18,... | collective-permute-start | bytes 221192 | tf_op jit(solution)/shard_map/ppermute | solution.py:302
  198.8 8.0 %collective-permute-start.7 = (f32[72,256]{1,0:T(8,128)S(1)}, f32[72,256]{1,0:T(8,128)S(1)}, u32[]{:S(2)}, u32[]{:S(2)}) collective-permute-start(f32[72,256]{1,0:T(8,128)S(1)} %add.42), channel_id=1, source_target_pairs={{0,6},{2,4},{4,2},{6,0},{8,14},{10,12},{12,10},{14,8},{16,22},{18,... | collective-permute-start | bytes 221192 | tf_op jit(solution)/shard_map/ppermute | solution.py:302
